TPU v7x, 256 devices: a whole 4x4x8 slice. The times are simulated.
256 devices in a mesh: span: 8 (over x, y_lo), tile: 32 (over z, y_hi, core).
Axes of the slice: x: 4, y: 4 (y_hi: 2, y_lo: 2; y = y_hi * 2 + y_lo), z: 8, core: 2. Of those that a mesh axis runs over, the one named last changes fastest.
Arguments:
- tokens: bfloat16 [8, 2304, 1536], P('span', 'tile'), may hold values from -6 to 6
- noise_steps: int32 [8], replicated, may hold values from 0 to 7, as said below
- span_mask: int32 [8, 8], replicated, may hold values from 0 to 1, as said below
- modulation: float32 [8, 5, 1536], replicated, may hold values from -3 to 3
- qkv_weight: bfloat16 [768, 9216], P(None, 'span'), may hold values from -1.5 to 1.5
- out_weight: bfloat16 [1536, 1536], P('span'), may hold values from -0.15625 to 0.15625
- head_weight: bfloat16 [768, 128], replicated, may hold values from -0.15625 to 0.15625
- head_bias: float32 [64], replicated, may hold values from -3 to 3
- frame_cache: bfloat16 [2, 64, 48, 16], P(None, 'tile'), may hold values from -6 to 6
- conv_weight: bfloat16 [432, 384], replicated, may hold values from -0.3125 to 0.3125
- conv_bias: float32 [384], replicated, may hold values from -3 to 3
Outputs:
- hidden_out: bfloat16 [8, 2304, 1536], P('span', 'tile')
- decoded_frames: bfloat16 [3, 64, 48, 384], P(None, 'tile', 'span')
Inputs may be any that keep to these rules, and one draw needn't show every extreme that they name: `noise_steps`: span 0, the finishing span, has level 0 and span 8 - 1 has level 7; the others lie in 1 to 7. `span_mask`: 1 on the diagonal, 0 above it, 0 or 1 below it.
All inputs are finite; a program needn't handle non-finite values.
Results may differ from a plain program's by a relative error of at most 0.015.
Values may be sent and summed in bfloat16 or wider, within the bound.
No kernel may reach another device: no remote copies, remote signals or barrier semaphores. Data moves between devices by JAX's collectives and lax.ppermute only.
A program may use at most 128 MiB of HBM per device.

v0:
```python
import jax
import jax.numpy as jnp
from jax import lax
from jax.sharding import PartitionSpec as P

HDIM = 64
LCH = 16
LF = 3
TROW_DEV = 1
TCOL = 24


epsilon = 1e-06
masked_score = -1e30


def with_halo(cells, sides, width):
    for axis, dim in sides:
        count = lax.axis_size(axis)
        ends = count - 1
        head = lax.slice_in_dim(cells, 0, width, axis=dim)
        tail = lax.slice_in_dim(cells, cells.shape[dim] - width, cells.shape[dim], axis=dim)
        cells = jnp.concatenate(
            [
                lax.ppermute(tail, axis, [(i, (i + 1) % count) for i in range(ends)]),
                cells,
                lax.ppermute(head, axis, [((i + 1) % count, i) for i in range(ends)]),
            ],
            axis=dim,
        )
    return cells


def from_root(block, axis, holder):
    block = jnp.where(lax.axis_index(axis) == holder, block, jnp.zeros_like(block))
    return lax.psum(block, axis)


def layer_norm(values):
    centred = values - jnp.mean(values, axis=-1, keepdims=True)
    spread = jnp.mean(centred * centred, axis=-1, keepdims=True)
    return centred * lax.rsqrt(spread + epsilon)


def convolve(padded, kernel, offsets, frame_count, row_count, col_count):
    pieces = []
    for frame_step in range(3):
        for row_step in range(3):
            for col_step in range(3):
                pieces.append(
                    padded[
                        frame_step : frame_step + frame_count,
                        row_step : row_step + row_count,
                        col_step : col_step + col_count,
                    ]
                )
    stacked = jnp.concatenate(pieces, axis=-1)
    product = jnp.dot(
        stacked.reshape(-1, stacked.shape[-1]), kernel, preferred_element_type=jnp.float32
    )
    return (product.reshape(frame_count, row_count, col_count, -1) + offsets).astype(jnp.bfloat16)


def per_device(
    tokens,
    noise_steps,
    span_mask,
    modulation,
    qkv_weight,
    out_weight,
    head_weight,
    head_bias,
    frame_cache,
    conv_weight,
    conv_bias,
):
    span_count = lax.axis_size("span")
    span_index = lax.axis_index("span")
    level_count = modulation.shape[0]
    picked = (noise_steps[:, None] == jnp.arange(level_count)[None, :]).astype(jnp.float32)
    per_span = jnp.einsum("cl,lkd->ckd", picked, modulation, precision=lax.Precision.HIGHEST)
    own_mod = lax.dynamic_index_in_dim(per_span, span_index, 0, keepdims=False)
    residual = tokens[0].astype(jnp.float32)
    tok_rows = residual.shape[0]
    normed = (layer_norm(residual) * (1.0 + own_mod[1]) + own_mod[0]).astype(jnp.bfloat16)
    half_rows = qkv_weight.shape[0]
    local_heads = qkv_weight.shape[1] // (6 * HDIM)
    local_width = local_heads * HDIM
    flat_weight = jnp.transpose(
        qkv_weight.reshape(half_rows, local_heads, 2, 3, HDIM), (0, 2, 3, 1, 4)
    ).reshape(2 * half_rows, 3 * local_width)
    projected = jnp.dot(
        lax.all_gather(normed, "span", axis=0, tiled=True),
        flat_weight,
        preferred_element_type=jnp.float32,
    ).astype(jnp.bfloat16)
    all_rows = projected.shape[0]
    queries = projected[:, :local_width].reshape(all_rows, local_heads, HDIM)
    key_rows = projected[:, local_width : 2 * local_width].reshape(
        span_count, tok_rows, local_width
    )
    value_rows = projected[:, 2 * local_width :].reshape(span_count, tok_rows, local_width)
    seen_spans = jnp.repeat(span_mask > 0, tok_rows, axis=0)
    score_scale = HDIM ** (-0.5)
    start_state = (
        jnp.full((local_heads, all_rows), masked_score, jnp.float32),
        jnp.zeros((local_heads, all_rows), jnp.float32),
        jnp.zeros((all_rows, local_heads, HDIM), jnp.float32),
    )
    key_piece = lax.all_gather(key_rows, "tile", axis=1, tiled=True)
    value_piece = lax.all_gather(value_rows, "tile", axis=1, tiled=True)
    piece_rows = key_piece.shape[1]
    block_rows = piece_rows
    while span_count * block_rows > 2048 and block_rows % 2 == 0:
        block_rows = block_rows // 2
    block_count = piece_rows // block_rows
    block_keys = span_count * block_rows
    key_blocks = jnp.transpose(
        key_piece.reshape(span_count, block_count, block_rows, local_heads, HDIM), (1, 0, 2, 3, 4)
    ).reshape(block_count, block_keys, local_heads, HDIM)
    value_blocks = jnp.transpose(
        value_piece.reshape(span_count, block_count, block_rows, local_heads, HDIM), (1, 0, 2, 3, 4)
    ).reshape(block_count, block_keys, local_heads, HDIM)
    allowed = jnp.repeat(seen_spans, block_rows, axis=1)

    def one_block(running, block_item):
        running_max, running_sum, weighted = running
        key_heads, value_heads = block_item
        scores = (
            jnp.einsum("qhd,khd->hqk", queries, key_heads, preferred_element_type=jnp.float32)
            * score_scale
        )
        scores = jnp.where(allowed[None, :, :], scores, masked_score)
        new_max = jnp.maximum(running_max, jnp.max(scores, axis=-1))
        rescale = jnp.exp(running_max - new_max)
        weights = jnp.where(allowed[None, :, :], jnp.exp(scores - new_max[:, :, None]), 0.0)
        running_sum = running_sum * rescale + jnp.sum(weights, axis=-1)
        blended = jnp.einsum(
            "hqk,khd->qhd",
            weights.astype(jnp.bfloat16),
            value_heads,
            preferred_element_type=jnp.float32,
        )
        weighted = weighted * jnp.transpose(rescale)[:, :, None] + blended
        return ((new_max, running_sum, weighted), None)

    folded, unused = lax.scan(one_block, start_state, (key_blocks, value_blocks))
    final_max, final_sum, final_weighted = folded
    merged = (
        (final_weighted / jnp.transpose(final_sum)[:, :, None])
        .astype(jnp.bfloat16)
        .reshape(all_rows, local_width)
    )
    projected_out = lax.psum_scatter(
        jnp.dot(merged, out_weight, preferred_element_type=jnp.float32).astype(jnp.bfloat16),
        "span",
        scatter_dimension=0,
        tiled=True,
    ).astype(jnp.float32)
    hidden = (residual + own_mod[2] * projected_out).astype(jnp.bfloat16)
    finish_mod = per_span[0]
    shaped = (
        layer_norm(hidden.astype(jnp.float32)) * (1.0 + finish_mod[4]) + finish_mod[3]
    ).astype(jnp.bfloat16)
    head_full = head_weight.reshape(2 * head_weight.shape[0], head_weight.shape[1] // 2)
    patches = (jnp.dot(shaped, head_full, preferred_element_type=jnp.float32) + head_bias).astype(
        jnp.bfloat16
    )
    latent = patches.reshape(LF, TROW_DEV, TCOL, 2, 2, LCH)
    latent = jnp.transpose(latent, (0, 1, 3, 2, 4, 5)).reshape(LF, 2 * TROW_DEV, 2 * TCOL, LCH)
    frames = jnp.concatenate([frame_cache, latent], axis=0)
    padded = with_halo(frames, (("tile", 1),), 1)
    padded = jnp.pad(padded, ((0, 0), (0, 0), (1, 1), (0, 0)))
    strip_rows = 2 * TROW_DEV
    slice_width = 2 * TCOL // span_count
    whole_strip = convolve(padded, conv_weight, conv_bias, LF, strip_rows, 2 * TCOL)
    whole_strip = from_root(whole_strip, "span", 0)
    decoded_frames = lax.dynamic_slice_in_dim(whole_strip, span_index * slice_width, slice_width, 2)
    return (hidden[None], decoded_frames)


def solution(mesh):
    in_specs = (
        P("span", "tile", None),
        P(),
        P(),
        P(),
        P(None, "span"),
        P("span", None),
        P(),
        P(),
        P(None, "tile", None, None),
        P(),
        P(),
    )
    out_specs = (P("span", "tile", None), P(None, "tile", "span", None))
    return jax.shard_map(
        per_device, mesh=mesh, in_specs=in_specs, out_specs=out_specs, check_vma=False
    )
```

profile of v0, /device:TPU:1, one launch (start us, length us, event | category | flops | bytes accessed | tf_op | source)
XLA Modules:
  0.0 752.0 jit_solution(9652505402966992320)
XLA Ops:
  21.1 7.8 %reshape.108 = bf16[1536,576]{1,0:T(8,128)(2,1)S(1)} reshape(bf16[768,2,3,3,64]{4,3,2,1,0:T(4,128)(2,1)} %copy.104) | data formatting | bytes 3538944 | tf_op jit(solution)/shard_map/reshape | solution.py:91
  29.0 34.3 %all-gather.4.cloned.1.call-done = bf16[576,1536]{1,0:T(8,128)(2,1)} async-done(((bf16[72,1536]{1,0:T(8,128)(2,1)}), bf16[576,1536]{1,0:T(8,128)(2,1)}) %all-gather.4.cloned.1.call-update) | async-done | bytes 1769488 | tf_op jit(solution)/shard_map/all_gather | solution.py:93
  68.8 107.2 %all-gather.6.cloned.1.call-done = bf16[8,2304,192]{2,1,0:T(8,128)(2,1)} async-done(((bf16[8,72,192]{2,1,0:T(8,128)(2,1)}), bf16[8,2304,192]{2,1,0:T(8,128)(2,1)}) %all-gather.6.cloned.1.call-update) | async-done | bytes 7077904 | tf_op jit(solution)/shard_map/all_gather | solution.py:110
  176.0 11.4 %copy.106 = bf16[8,2304,192]{1,2,0:T(8,128)(2,1)} copy(bf16[8,2304,192]{2,1,0:T(8,128)(2,1)} %all-gather.6.cloned.1.call-done) | data formatting | bytes 14155776 | tf_op jit(solution)/shard_map/all_gather | solution.py:110
  187.4 23.0 %reshape.110 = bf16[8,16,144,3,64]{2,1,4,3,0:T(8,128)(2,1)} reshape(bf16[8,2304,192]{1,2,0:T(8,128)(2,1)} %copy.106) | data formatting | bytes 14155776 | tf_op jit(solution)/shard_map/reshape | solution.py:119
  210.4 14.1 %copy.107 = bf16[16,8,144,3,64]{2,1,4,3,0:T(8,128)(2,1)} copy(bf16[16,8,144,3,64]{2,0,4,3,1:T(8,128)(2,1)} %bitcast.115) | data formatting | bytes 14155776 | tf_op jit(solution)/shard_map/transpose | solution.py:118
  224.5 19.4 %reshape.111 = bf16[16,1152,3,64]{1,3,2,0:T(8,128)(2,1)} reshape(bf16[16,8,144,3,64]{2,1,4,3,0:T(8,128)(2,1)} %copy.107) | data formatting | bytes 14155776 | tf_op jit(solution)/shard_map/reshape | solution.py:120
  243.9 37.5 %all-gather.8.cloned.1.call-done = bf16[8,2304,192]{2,1,0:T(8,128)(2,1)} async-done(((bf16[8,72,192]{2,1,0:T(8,128)(2,1)}), bf16[8,2304,192]{2,1,0:T(8,128)(2,1)}) %all-gather.8.cloned.1.call-update) | async-done | bytes 7077904 | tf_op jit(solution)/shard_map/all_gather | solution.py:111
  281.4 11.4 %copy.109 = bf16[8,2304,192]{1,2,0:T(8,128)(2,1)} copy(bf16[8,2304,192]{2,1,0:T(8,128)(2,1)} %all-gather.8.cloned.1.call-done) | data formatting | bytes 14155776 | tf_op jit(solution)/shard_map/all_gather | solution.py:111
  292.8 23.0 %reshape.114 = bf16[8,16,144,3,64]{2,1,4,3,0:T(8,128)(2,1)} reshape(bf16[8,2304,192]{1,2,0:T(8,128)(2,1)} %copy.109) | data formatting | bytes 14155776 | tf_op jit(solution)/shard_map/reshape | solution.py:122
  315.8 14.1 %copy.110 = bf16[16,8,144,3,64]{2,1,4,3,0:T(8,128)(2,1)} copy(bf16[16,8,144,3,64]{2,0,4,3,1:T(8,128)(2,1)} %bitcast.116) | data formatting | bytes 14155776 | tf_op jit(solution)/shard_map/transpose | solution.py:121
  329.9 19.3 %reshape.115 = bf16[16,1152,3,64]{1,3,2,0:T(8,128)(2,1)} reshape(bf16[16,8,144,3,64]{2,1,4,3,0:T(8,128)(2,1)} %copy.110) | data formatting | bytes 14155776 | tf_op jit(solution)/shard_map/reshape | solution.py:123
  349.2 258.2 %while.15 = (s32[]{:T(128)}, f32[3,576]{1,0:T(4,128)S(1)}, f32[3,576]{1,0:T(4,128)S(1)}, f32[576,3,64]{0,2,1:T(8,128)S(1)}, bf16[16,1152,3,64]{1,3,2,0:T(8,128)(...) while((s32[]{:T(128)}, f32[3,576]{1,0:T(4,128)S(1)}, ...), condition=%wide.region_5.6_spmd.clone, body=%wide.region_2.5_spmd.clone.sunk | while | flops 535828608 | bytes 61826696 | solution.py:147
  357.0 5.9 fusion.91
  373.1 5.9 fusion.91
  389.2 5.9 fusion.91
  405.3 5.9 fusion.91
  421.5 5.9 fusion.91
  437.6 5.9 fusion.91
  453.7 5.9 fusion.91
  469.8 5.9 fusion.91
  486.0 5.9 fusion.91
  502.1 5.9 fusion.91
  518.2 5.9 fusion.91
  534.3 5.9 fusion.91
  550.5 5.9 fusion.91
  566.6 5.9 fusion.91
  582.7 5.9 fusion.91
  598.9 5.9 fusion.91
  609.8 43.1 %reduce-scatter.2.cloned.1.call-done = bf16[72,1536]{1,0:T(8,128)(2,1)} async-done(((bf16[576,1536]{1,0:T(8,128)(2,1)}), bf16[72,1536]{1,0:T(8,128)(2,1)}) %reduce-scatter.2.cloned.1.call-update) | async-done | bytes 221200 | tf_op jit(solution)/shard_map/reduce_scatter | solution.py:154
  654.9 6.9 collective-permute-start
  671.4 72.5 %all-reduce.3.cloned.1.call-done = bf16[3,2,48,384]{3,2,1,0:T(8,128)(2,1)} async-done(((bf16[3,2,48,384]{3,2,1,0:T(8,128)(2,1)}), bf16[3,2,48,384]{3,2,1,0:T(8,128)(2,1)}) %all-reduce.3.cloned.1.call-update) | async-done | bytes 221200 | tf_op jit(solution)/shard_map/psum | solution.py:36
  (216 shorter events, 197.6 us)
Async XLA Ops:
  7.2 600.4 %copy-start = (bf16[192,1536]{1,0:T(8,128)(2,1)S(1)}, bf16[192,1536]{1,0:T(8,128)(2,1)}, u32[]{:S(2)}) copy-start(bf16[192,1536]{1,0:T(8,128)(2,1)} %param.18) | copy-start | bytes 1769476
  7.2 56.1 %all-gather.4.cloned.1.call-start = ((), (), s32[]{:S(2)}) async-start(), calls=%async_computation.1 | async-start | bytes 1990656 | tf_op jit(solution)/shard_map/all_gather | solution.py:93
  12.7 163.2 %all-gather.6.cloned.1.call-start = ((), (), s32[]{:S(2)}) async-start(), calls=%async_computation.2 | async-start | bytes 9732096 | tf_op jit(solution)/shard_map/all_gather | solution.py:110
  29.0 39.5 %copy-start.6 = (s32[8,8]{1,0:T(8,128)S(1)}, s32[8,8]{1,0:T(8,128)}, u32[]{:S(2)}) copy-start(s32[8,8]{1,0:T(8,128)} %param.15) | copy-start | bytes 772
  67.3 214.1 %all-gather.8.cloned.1.call-start = ((), (), s32[]{:S(2)}) async-start(), calls=%async_computation.3 | async-start | bytes 9732096 | tf_op jit(solution)/shard_map/all_gather | solution.py:111
  68.2 584.7 %reduce-scatter.2.cloned.1.call-start = ((), (), s32[]{:S(2)}) async-start(), calls=%async_computation.4 | async-start | bytes 1990656 | tf_op jit(solution)/shard_map/reduce_scatter | solution.py:154
  349.2 260.3 %copy-start.4 = (bf16[768,128]{1,0:T(8,128)(2,1)S(1)}, bf16[768,128]{1,0:T(8,128)(2,1)}, u32[]{:S(2)}) copy-start(bf16[768,128]{1,0:T(8,128)(2,1)} %param.19) | copy-start | bytes 589828
  349.2 260.5 %copy-start.5 = (bf16[2,2,48,16]{2,3,1,0:T(8,128)(2,1)S(1)}, bf16[2,2,48,16]{2,3,1,0:T(8,128)(2,1)}, u32[]{:S(2)}) copy-start(bf16[2,2,48,16]{2,3,1,0:T(8,128)(2,1)} %param.21) | copy-start | bytes 18436
  349.2 303.8 %copy-start.2 = (bf16[1,72,1536]{2,1,0:T(8,128)(2,1)S(1)}, bf16[1,72,1536]{2,1,0:T(8,128)(2,1)}, u32[]{:S(2)}) copy-start(bf16[1,72,1536]{2,1,0:T(8,128)(2,1)} %param.13) | copy-start | bytes 663556
  349.2 305.1 %copy-start.9 = (f32[64]{0:T(128)S(1)}, f32[64]{0:T(128)}, u32[]{:S(2)}) copy-start(f32[64]{0:T(128)} %param.20) | copy-start | bytes 772
  357.0 5.9 copy-start.1
  373.1 5.9 copy-start.1
  389.2 5.9 copy-start.1
  405.3 5.9 copy-start.1
  421.5 5.9 copy-start.1
  437.6 5.9 copy-start.1
  453.7 5.9 copy-start.1
  469.8 5.9 copy-start.1
  486.0 5.9 copy-start.1
  502.1 5.9 copy-start.1
  518.2 5.9 copy-start.1
  534.3 5.9 copy-start.1
  550.5 5.9 copy-start.1
  566.6 5.9 copy-start.1
  582.7 5.9 copy-start.1
  598.8 5.9 copy-start.1
  607.4 62.9 %copy-start.7 = (bf16[432,384]{1,0:T(8,128)(2,1)S(1)}, bf16[432,384]{1,0:T(8,128)(2,1)}, u32[]{:S(2)}) copy-start(bf16[432,384]{1,0:T(8,128)(2,1)} %param.22) | copy-start | bytes 995332
  607.5 62.9 %copy-start.8 = (f32[384]{0:T(512)S(1)}, f32[384]{0:T(512)}, u32[]{:S(2)}) copy-start(f32[384]{0:T(512)} %param.23) | copy-start | bytes 4612
  609.4 134.5 %all-reduce.3.cloned.1.call-start = ((), (), s32[]{:S(2)}) async-start(), calls=%async_computation.5 | async-start | bytes 442368 | tf_op jit(solution)/shard_map/psum | solution.py:36
  654.1 91.4 %copy-start.3 = (bf16[72,1536]{1,0:T(8,128)(2,1)}, bf16[72,1536]{1,0:T(8,128)(2,1)S(1)}, u32[]{:S(2)}) copy-start(bf16[72,1536]{1,0:T(8,128)(2,1)S(1)} %get-tuple-element.115) | copy-start | bytes 663556
  654.9 8.9 %collective-permute-start = (bf16[5,1,48,16]{3,2,1,0:T(8,128)(2,1)S(1)}, bf16[5,1,48,16]{3,2,1,0:T(8,128)(2,1)S(1)}, u32[]{:S(2)}, u32[]{:S(2)}) collective-permute-start(bf16[5,1,48,16]{3,2,1,0:T(8,128)(2,1)S(1)} %get-tuple-element.149), channel_id=1, source_target_pairs={{0,1},{1,2},{2,3},{3,4},{4,5},{5,6},{6,7},{7,8},{8,9},{9,10},{10,1... | collective-permute-start | bytes 23048 | tf_op jit(solution)/shard_map/ppermute | solution.py:25
  661.9 7.0 collective-permute-start.1
Sparse Core Ops, SparseCore 0:
  12.8 50.3 all-gather.3
  67.4 108.5 all-gather.5
  178.7 102.6 all-gather.7
  609.6 43.3 reduce-scatter.1
  671.5 72.3 all-reduce.2
where the time goes:
time: 760 us; the launch traced here: 752 us
  waiting for transfers between devices  300 us (39%)
  matrix products  195 us (26%)
  local copies, waits for them, and re-layouts  183 us (24%)
  other arithmetic  48.9 us (6%)
  between operations  14.1 us (2%)
  starting transfers between devices  9.24 us (1%)
    all_gather x1, waiting for transfers between devices, per_device(): key_piece = lax.all_gather(key_rows, 'tile', axis=1, tiled=True)  107 us
    dot_general x16, matrix products, one_block(): jnp.einsum('hqk,khd->qhd', weights.astype(jnp.bfloat16), value_heads, pre...  93.9 us
    dot_general x16, matrix products, one_block(): jnp.einsum('qhd,khd->hqk', queries, key_heads, preferred_element_type=jnp...  93.9 us
    psum x1, waiting for transfers between devices, from_root(): return lax.psum(block, axis)  72.5 us
    reduce_scatter x1, waiting for transfers between devices, per_device(): lax.psum_scatter(jnp.dot(merged, out_weight, preferred_element_type=jnp.f...  43.1 us
    reduce_sum x16, other arithmetic, one_block(): running_sum = running_sum * rescale + jnp.sum(weights, axis=-1)  42.6 us
    all_gather x1, waiting for transfers between devices, per_device(): value_piece = lax.all_gather(value_rows, 'tile', axis=1, tiled=True)  37.5 us
    all_gather x1, waiting for transfers between devices, per_device(): lax.all_gather(normed, 'span', axis=0, tiled=True)  34.3 us
  transfers between devices with their start and end apart: 7, of which 6 were waited for; matrix products, arithmetic and copies ran while one was open for 11% of the time, Pallas kernels for 0%

commit v1 on v0

v1 whole, which is shorter than its diff:
```python
import functools

import jax
import jax.numpy as jnp
from jax import lax
from jax.experimental import pallas as pl
from jax.experimental.pallas import tpu as pltpu
from jax.sharding import Mesh
from jax.sharding import PartitionSpec as P

HDIM = 64
LCH = 16
LF = 3
TCOL = 24
D = 1536
SPANS = 8
ROWS = 72
VCH = 384
GROUP = 3
LANES = 256
KVW = 384
EPS = 1e-06
LOW = -1e30
SPAN = ("x", "ylo")
TILE = ("z", "yhi", "core")
VMEM_LIMIT = 48 * 1024 * 1024

bf16 = jnp.bfloat16
f32 = jnp.float32


def shift(block, axis, count, step):
    return lax.ppermute(block, axis, [(i, (i + step) % count) for i in range(count)])


def normalise(values):
    centred = values - jnp.mean(values, axis=-1, keepdims=True)
    spread = jnp.mean(centred * centred, axis=-1, keepdims=True)
    return centred * lax.rsqrt(spread + EPS)


def qkv_kernel(place, levels, mod, perm, weight, *refs):
    tokens = refs[:SPANS]
    q_ref, kv_ref, normed = refs[SPANS:]
    me = place[0]
    for step in range(SPANS):
        span = lax.rem(me - step + SPANS, SPANS)
        level = levels[span]
        values = normalise(tokens[step][...].astype(f32))
        values = values * (1.0 + mod[level, 1:2, :]) + mod[level, 0:1, :]
        normed[step * ROWS : (step + 1) * ROWS, :] = values
    total = jnp.zeros((SPANS * ROWS, LANES + KVW), f32)
    for block in range(D // 256):
        part = normed[:, block * 256 : (block + 1) * 256].astype(bf16)
        part = jnp.dot(part, perm[...], preferred_element_type=f32).astype(bf16)
        total += jnp.dot(
            part, weight[block * 256 : (block + 1) * 256, :], preferred_element_type=f32
        )
    for step in range(SPANS):
        span = lax.rem(me - step + SPANS, SPANS)
        rows = total[step * ROWS : (step + 1) * ROWS, :].astype(bf16)
        q_ref[span] = rows[:, :LANES] * jnp.asarray(HDIM**-0.5, bf16)
        kv_ref[span] = rows[:, LANES:]


def arrange_kernel(raw, out):
    width = LANES + KVW
    row = lax.broadcasted_iota(jnp.int32, (256, width), 0)
    col = lax.broadcasted_iota(jnp.int32, (256, width), 1) - HDIM
    kind = col // (GROUP * HDIM)
    head = (col % (GROUP * HDIM)) // HDIM
    source = jnp.where(kind == 0, 0, 3 - kind) * HDIM + col % HDIM
    for parity in range(2):
        total = jnp.zeros((D // 2, width), f32)
        for group in range(GROUP):
            begin = group * 2 * KVW // 2 + parity * 128
            wanted = (row == source + parity * HDIM) & (head == group) & (col >= 0)
            total += jnp.dot(
                raw[:, begin : begin + 256],
                jnp.where(wanted, 1.0, 0.0).astype(bf16),
                preferred_element_type=f32,
            )
        for block in range(D // 256):
            out[block * 256 + parity * 128 : block * 256 + parity * 128 + 128, :] = total[
                block * 128 : (block + 1) * 128
            ].astype(bf16)


def arrange(raw):
    vmem = pl.BlockSpec(memory_space=pltpu.VMEM)
    return pl.pallas_call(
        arrange_kernel,
        out_shape=jax.ShapeDtypeStruct((D, LANES + KVW), bf16),
        in_specs=[vmem],
        out_specs=vmem,
        compiler_params=pltpu.CompilerParams(vmem_limit_bytes=VMEM_LIMIT),
        cost_estimate=pl.CostEstimate(
            flops=4000000000, bytes_accessed=4000000, transcendentals=0
        ),
        name="arrange",
    )(raw)


def project_spans(place, levels, modulation, weight, blocks):
    row = jnp.arange(256)
    perm = (row[:, None] == (2 * (row % 128) + row // 128)[None, :]).astype(bf16)
    smem = pl.BlockSpec(memory_space=pltpu.SMEM)
    vmem = pl.BlockSpec(memory_space=pltpu.VMEM)
    return pl.pallas_call(
        qkv_kernel,
        out_shape=(
            jax.ShapeDtypeStruct((SPANS, ROWS, LANES), bf16),
            jax.ShapeDtypeStruct((SPANS, ROWS, KVW), bf16),
        ),
        in_specs=[smem, smem] + [vmem] * (3 + SPANS),
        out_specs=(vmem, vmem),
        scratch_shapes=[pltpu.VMEM((SPANS * ROWS, D), f32)],
        compiler_params=pltpu.CompilerParams(vmem_limit_bytes=VMEM_LIMIT),
        cost_estimate=pl.CostEstimate(
            flops=2 * SPANS * ROWS * D * 640, bytes_accessed=4500000, transcendentals=0
        ),
        name="qkv",
    )(place, levels, modulation, perm, weight, *blocks)


def split_bf16(value, count):
    parts = []
    for _ in range(count):
        part = value.astype(bf16).astype(f32)
        parts.append(part)
        value = value - part
    return parts


def attend_kernel(
    place, mask, qa, qb, kv, out, pairs, queries, keys, values, s0, s1, p0, p1, r0, r1, acc, peak
):
    step = pl.program_id(0)
    count = kv.shape[0] * ROWS
    rows = 2 * ROWS
    stack = GROUP * rows
    lane = lax.broadcasted_iota(jnp.int32, (1, LANES), 1)

    @pl.when(step == 0)
    def _():
        for span in range(SPANS):
            both = jnp.concatenate([qa[span].astype(f32), qb[span].astype(f32)], axis=0)
            for head in range(GROUP):
                queries[span, head * rows : (head + 1) * rows, :] = jnp.where(
                    lane // HDIM == head + 1, both, 0.0
                ).astype(bf16)
        queries[SPANS] = jnp.zeros((stack, LANES), bf16)
        acc[...] = jnp.zeros_like(acc)
        peak[...] = jnp.full_like(peak, LOW)
        p0[...] = jnp.zeros_like(p0)
        r0[...] = jnp.zeros_like(r0)

    block = kv[:, 0].astype(f32).reshape(count, KVW)
    values[step] = jnp.where(lane // HDIM == 3, 1.0, block[:, :LANES]).astype(bf16)
    keys[step] = block[:, KVW - LANES :].astype(bf16)

    def put(index, span, key_span):
        pairs[2 * index] = span
        pairs[2 * index + 1] = key_span

    def score(index, scores):
        scores[...] = lax.dot_general(
            queries[pairs[2 * index]],
            keys[pairs[2 * index + 1]],
            (((1,), (1,)), ((), ())),
            preferred_element_type=f32,
        )

    def weigh(index, scores, probs, rescale):
        span = pairs[2 * index]
        old = peak[span, :, 0:1]
        block = scores[...]
        new = jnp.maximum(old, jnp.max(block, axis=1, keepdims=True))
        probs[...] = jnp.exp(block - new).astype(bf16)
        peak[span] = jnp.broadcast_to(new, (stack, 128))
        rescale[...] = jnp.broadcast_to(jnp.exp(old - new), (stack, 128))

    def blend(index, probs, rescale):
        span = pairs[2 * index]
        acc[span] = acc[span] * rescale[:, 0:1] + jnp.dot(
            probs[...], values[pairs[2 * index + 1]], preferred_element_type=f32
        )

    @pl.when(step == SPANS - 1)
    def _():
        put(0, SPANS, 0)

        def scan(at, found):
            span, key_span = at // SPANS, at % SPANS
            seen = mask[span, key_span] > 0

            @pl.when(seen)
            def _():
                put(found, span, key_span)

            return jnp.where(seen, found + 1, found)

        found = lax.fori_loop(0, SPANS * SPANS, scan, jnp.int32(1))
        for extra in range(4):
            put(found + extra, SPANS, 0)
        score(1, s1)

        def both_slots(trip, carry):
            at = 2 * trip + 1
            score(at + 1, s0)
            weigh(at, s1, p1, r1)
            blend(at - 1, p0, r0)
            score(at + 2, s1)
            weigh(at + 1, s0, p0, r0)
            blend(at, p1, r1)
            return carry

        lax.fori_loop(0, (found + 1) // 2, both_slots, 0)

        mine = place[1]
        for span in range(SPANS):
            heads = [acc[span, head * rows : (head + 1) * rows, :] for head in range(GROUP)]
            merged = jnp.where(lane < HDIM, heads[0], jnp.where(lane < 2 * HDIM, heads[1], heads[2]))
            columns = []
            for head in range(GROUP):
                columns += split_bf16(peak[span, head * rows : (head + 1) * rows, 0:1], 3)
                columns += split_bf16(heads[head][:, 192:193], 2)
            for index, column in enumerate(columns):
                merged = jnp.where(lane == 192 + index, column, merged)
            out[span, mine] = merged[:ROWS].astype(bf16)
            out[span, 1 - mine] = merged[ROWS:].astype(bf16)


def attend(place, mask, qa, qb, kv):
    sources = kv.shape[0]
    smem = pl.BlockSpec(memory_space=pltpu.SMEM)
    vmem = pl.BlockSpec(memory_space=pltpu.VMEM)
    stack = 2 * ROWS * GROUP
    count = sources * ROWS
    return pl.pallas_call(
        attend_kernel,
        grid=(SPANS,),
        out_shape=jax.ShapeDtypeStruct((SPANS, 2, ROWS, LANES), bf16),
        in_specs=[
            smem,
            smem,
            vmem,
            vmem,
            pl.BlockSpec((sources, 1, ROWS, KVW), lambda i: (0, i, 0, 0)),
        ],
        out_specs=pl.BlockSpec((SPANS, 2, ROWS, LANES), lambda i: (0, 0, 0, 0)),
        scratch_shapes=[
            pltpu.SMEM((2 * (SPANS * SPANS + 8),), jnp.int32),
            pltpu.VMEM((SPANS + 1, stack, LANES), bf16),
            pltpu.VMEM((SPANS, count, LANES), bf16),
            pltpu.VMEM((SPANS, count, LANES), bf16),
            pltpu.VMEM((stack, count), f32),
            pltpu.VMEM((stack, count), f32),
            pltpu.VMEM((stack, count), bf16),
            pltpu.VMEM((stack, count), bf16),
            pltpu.VMEM((stack, 128), f32),
            pltpu.VMEM((stack, 128), f32),
            pltpu.VMEM((SPANS + 1, stack, LANES), f32),
            pltpu.VMEM((SPANS + 1, stack, 128), f32),
        ],
        compiler_params=pltpu.CompilerParams(
            vmem_limit_bytes=VMEM_LIMIT, dimension_semantics=("arbitrary",)
        ),
        cost_estimate=pl.CostEstimate(
            flops=8000000000, bytes_accessed=8000000, transcendentals=12000000
        ),
        name="attend",
    )(place, mask, qa, qb, kv)


def finish_kernel(
    place, levels, parts, near, far, tokens, mod, head_full, bias, hidden, patches, weight
):
    lane = lax.broadcasted_iota(jnp.int32, (HDIM, LANES), 1)
    slot = lax.broadcasted_iota(jnp.int32, (HDIM, LANES), 0)
    head = lane // HDIM
    peaks = jnp.where((slot >= head * 5) & (slot < head * 5 + 3) & (head < 3), 1.0, 0.0).astype(bf16)
    sums = jnp.where((slot >= head * 5 + 3) & (slot < head * 5 + 5) & (head < 3), 1.0, 0.0).astype(
        bf16
    )
    total = jnp.zeros((ROWS, D), f32)
    core = place[2]
    for step in range(SPANS):
        group = lax.rem(place[0] - step + SPANS, SPANS)
        weight[:96, :] = jnp.where(core == 0, near[step], far[step])
        weight[96:, :] = jnp.where(core == 0, far[step], near[step])
        tops, totals, outs = [], [], []
        for half in range(2):
            part = parts[group * 2 + half]
            tops.append(jnp.dot(part[:, 192:], peaks, preferred_element_type=f32))
            totals.append(jnp.dot(part[:, 192:], sums, preferred_element_type=f32))
            outs.append(part.astype(f32))
        top = jnp.maximum(tops[0], tops[1])
        scale = [jnp.exp(tops[0] - top), jnp.exp(tops[1] - top)]
        blended = (outs[0] * scale[0] + outs[1] * scale[1]) / (
            totals[0] * scale[0] + totals[1] * scale[1]
        )
        total += jnp.dot(
            blended[:, :192].astype(bf16),
            weight[...],
            preferred_element_type=f32,
        )
    level = levels[place[0]]
    result = (tokens[...].astype(f32) + mod[level, 2:3, :] * total).astype(bf16)
    hidden[...] = result
    first = levels[0]
    shaped = normalise(result.astype(f32)) * (1.0 + mod[first, 4:5, :]) + mod[first, 3:4, :]
    patches[...] = (
        jnp.dot(shaped.astype(bf16), head_full[...], preferred_element_type=f32) + bias[...]
    ).astype(bf16)


def finish(place, levels, parts, near, far, tokens, modulation, head_full, bias):
    smem = pl.BlockSpec(memory_space=pltpu.SMEM)
    vmem = pl.BlockSpec(memory_space=pltpu.VMEM)
    return pl.pallas_call(
        finish_kernel,
        out_shape=(
            jax.ShapeDtypeStruct((ROWS, D), bf16),
            jax.ShapeDtypeStruct((ROWS, 4 * LCH), bf16),
        ),
        in_specs=[smem, smem] + [vmem] * 7,
        out_specs=(vmem, vmem),
        scratch_shapes=[pltpu.VMEM((192, D), bf16)],
        compiler_params=pltpu.CompilerParams(vmem_limit_bytes=VMEM_LIMIT),
        cost_estimate=pl.CostEstimate(
            flops=2 * ROWS * D * D, bytes_accessed=6000000, transcendentals=0
        ),
        name="finish",
    )(place, levels, parts, near, far, tokens, modulation, head_full, bias)


def per_device(
    tokens,
    noise_steps,
    span_mask,
    modulation,
    qkv_weight,
    out_weight,
    head_weight,
    head_bias,
    frame_cache,
    conv_weight,
    conv_bias,
):
    span = lax.axis_index(SPAN)
    yhi = lax.axis_index("yhi")
    core = lax.axis_index("core")
    place = jnp.stack([span, yhi, core]).astype(jnp.int32)
    own = tokens[0]

    blocks = [own] + [shift(own, SPAN, SPANS, step) for step in range(1, SPANS)]

    weight = arrange(qkv_weight)
    q_own, kv_own = project_spans(place, noise_steps, modulation, weight, blocks)

    kv = lax.all_gather(kv_own, ("z", "core"))
    q_other = shift(q_own, "yhi", 2, 1)

    half = lax.dynamic_slice_in_dim(out_weight, core * 96, 96, 0)
    half, _ = lax.optimization_barrier((half, q_own))
    halves = [half] + [shift(half, SPAN, SPANS, step) for step in range(1, SPANS)]
    stacked = jnp.stack(halves)
    other = shift(stacked, "core", 2, 1)
    partial = attend(place, span_mask, q_own, q_other, kv)
    parts = lax.all_to_all(
        partial.reshape(2 * SPANS, ROWS, LANES), SPAN + ("yhi",), 0, 0
    )
    hidden, patches = finish(
        place,
        noise_steps,
        parts,
        stacked,
        other,
        own,
        modulation,
        head_weight.reshape(D, 4 * LCH),
        head_bias[None, :],
    )

    spread = lax.all_to_all(jnp.broadcast_to(patches[None], (SPANS,) + patches.shape), SPAN, 0, 0)
    latent = spread[0].reshape(LF, TCOL, 2, 2, LCH)
    latent = jnp.transpose(latent, (0, 2, 1, 3, 4)).reshape(LF, 2, 2 * TCOL, LCH)
    frames = jnp.concatenate([frame_cache, latent], axis=0)
    up = [(i, i + 1) for i in range(31)]
    down = [(i + 1, i) for i in range(31)]
    above = lax.ppermute(frames[:, 1:2], TILE, up)
    below = lax.ppermute(frames[:, 0:1], TILE, down)
    padded = jnp.concatenate([above, frames, below], axis=1)
    padded = jnp.pad(padded, ((0, 0), (0, 0), (1, 1), (0, 0)))
    mine = lax.dynamic_slice_in_dim(padded, span * 6, 8, axis=2)
    pieces = []
    for a in range(3):
        for b in range(3):
            for e in range(3):
                pieces.append(mine[a : a + 3, b : b + 2, e : e + 6])
    cells = jnp.concatenate(pieces, axis=-1).reshape(36, 27 * LCH)
    product = jnp.dot(cells, conv_weight, preferred_element_type=f32) + conv_bias
    decoded = product.astype(bf16).reshape(3, 2, 6, VCH)
    return (hidden[None], decoded)


def solution(mesh):
    fine = Mesh(mesh.devices.reshape(4, 2, 8, 2, 2), SPAN + TILE)
    in_specs = (
        P(SPAN, TILE, None),
        P(),
        P(),
        P(),
        P(None, SPAN),
        P(SPAN, None),
        P(),
        P(),
        P(None, TILE, None, None),
        P(),
        P(),
    )
    out_specs = (P(SPAN, TILE, None), P(None, TILE, SPAN, None))
    return jax.shard_map(
        per_device, mesh=fine, in_specs=in_specs, out_specs=out_specs, check_vma=False
    )
```

time: 760 us -> 183 us (0.24)
  waiting for transfers between devices: 300 us -> 47.4 us
  matrix products: 195 us -> 0.18 us
  local copies, waits for them, and re-layouts: 183 us -> 13.7 us
  other arithmetic: 48.9 us -> 0.27 us
  starting transfers between devices: 9.24 us -> 54.5 us
  Pallas kernels: 0 us -> 42.1 us
  blocking collectives: 0 us -> 8.62 us
    dot_general x37 -> x1, matrix products: 195 us -> 0.18 us  [per_device(): jnp.dot(cells, conv_weight, preferred_element_type=f32) + conv_bias]
    all_gather x3 -> x1, waiting for transfers between devices: 179 us -> 3.04 us  [per_device(): kv = lax.all_gather(kv_own, ('z', 'core'))]
    reshape x8 -> x4, local copies, waits for them, and re-layouts: 92.9 us -> 1.1 us  [the longest x1 0.96 us: per_device(): head_weight.reshape(D, 4 * LCH)]
    psum x1 -> x0, waiting for transfers between devices: 72.5 us -> none  [from_root(): return lax.psum(block, axis)]
    reduce_sum x20 -> x0, other arithmetic: 46.2 us -> none  [the longest x16 42.6 us: one_block(): running_sum = running_sum * rescale + jnp.sum(weights, axis=-1)]
    reduce_scatter x1 -> x0, waiting for transfers between devices: 43.1 us -> none  [per_device(): lax.psum_scatter(jnp.dot(merged, out_weight, preferred_element_type=jnp.f...]
    pallas_call x0 -> x4, Pallas kernels: none -> 42.1 us  [the longest x1 30.6 us: attend(): pl.pallas_call(attend_kernel, grid=(SPANS,), out_shape=jax.ShapeDtypeStru...]
    ppermute x2 -> x18, starting transfers between devices: 8.85 us -> 47.9 us  [the longest x16 39.8 us: shift(): lax.ppermute(block, axis, [(i, (i + step) % count) for i in range(count)])]
  transfers between devices with their start and end apart: 7 -> 20, of which waited for: 6 -> 9; matrix products, arithmetic and copies ran while one was open for 11% -> 1% of each run, Pallas kernels for 0% -> 18%
where the time goes in v1:
time: 183 us; the launch traced here: 181 us
  starting transfers between devices  54.5 us (30%)
  waiting for transfers between devices  47.4 us (26%)
  Pallas kernels  42.1 us (23%)
  between operations  14.5 us (8%)
  local copies, waits for them, and re-layouts  13.7 us (7%)
  blocking collectives  8.62 us (5%)
    ppermute x16, starting transfers between devices, shift(): lax.ppermute(block, axis, [(i, (i + step) % count) for i in range(count)])  39.8 us
    ppermute x16, waiting for transfers between devices, shift(): lax.ppermute(block, axis, [(i, (i + step) % count) for i in range(count)])  32.7 us
    pallas_call x1, Pallas kernels, attend(): pl.pallas_call(attend_kernel, grid=(SPANS,), out_shape=jax.ShapeDtypeStru...  30.6 us
    unnamed x73, local copies, waits for them, and re-layouts  11.8 us
    all_to_all x1, waiting for transfers between devices, per_device(): lax.all_to_all(partial.reshape(2 * SPANS, ROWS, LANES), SPAN + ('yhi',),...  10.7 us
    all_to_all x1, blocking collectives, per_device(): lax.all_to_all(jnp.broadcast_to(patches[None], (SPANS,) + patches.shape),...  8.62 us
    all_to_all x1, starting transfers between devices, per_device(): lax.all_to_all(partial.reshape(2 * SPANS, ROWS, LANES), SPAN + ('yhi',),...  6.58 us
    pallas_call x1, Pallas kernels, finish(): pl.pallas_call(finish_kernel, out_shape=(jax.ShapeDtypeStruct((ROWS, D),...  5.11 us
  transfers between devices with their start and end apart: 20, of which 9 were waited for; matrix products, arithmetic and copies ran while one was open for 1% of the time, Pallas kernels for 18%

profile of v1, /device:TPU:1, one launch (start us, length us, event | category | flops | bytes accessed | tf_op | source)
XLA Modules:
  0.0 181.3 jit_solution(2242070891788867733)
XLA Ops:
  7.2 2.2 %collective-permute-start = (bf16[72,1536]{1,0:T(8,128)(2,1)}, bf16[72,1536]{1,0:T(8,128)(2,1)S(1)}, u32[]{:S(2)}, u32[]{:S(2)}) collective-permute-start(bf16[72,1536]{1,0:T(8,128)(2,1)} %bitcast.30), channel_id=1, source_target_pairs={{0,32},{32,64},{64,96},{96,128},{128,160},{160,192},{192,224},{224... | collective-permute-start | bytes 663560 | tf_op jit(solution)/shard_map/ppermute | solution.py:33
  9.4 1.2 collective-permute-start.1
  10.6 1.7 collective-permute-start.2
  12.4 1.7 collective-permute-start.3
  14.1 2.9 %collective-permute-start.4 = (bf16[72,1536]{1,0:T(8,128)(2,1)}, bf16[72,1536]{1,0:T(8,128)(2,1)}, u32[]{:S(2)}, u32[]{:S(2)}) collective-permute-start(bf16[72,1536]{1,0:T(8,128)(2,1)} %bitcast.34), channel_id=1, source_target_pairs={{0,160},{32,192},{64,224},{96,0},{128,32},{160,64},{192,96},{224,1... | collective-permute-start | bytes 663560 | tf_op jit(solution)/shard_map/ppermute | solution.py:33
  17.0 1.1 copy.64.mod
  18.1 1.5 copy-done.8
  19.5 2.1 %arrange.1.weight = bf16[1536,640]{1,0:T(8,128)(2,1)S(1)} custom-call(bf16[768,1152]{1,0:T(8,128)(2,1)S(1)} %copy-done.8), custom_call_target="tpu_custom_call" | custom-call | flops 4000000000 | bytes 4000000 | tf_op jit(solution)/shard_map/arrange/pallas_call | solution.py:91
  21.7 1.2 collective-permute-start.5
  23.0 5.4 %collective-permute-done.2.refs_3_ = bf16[72,1536]{1,0:T(8,128)(2,1)} collective-permute-done((bf16[72,1536]{1,0:T(8,128)(2,1)}, bf16[72,1536]{1,0:T(8,128)(2,1)}, u32[]{:S(2)}, u32[]{:S(2)}) %collective-permute-start.2) | collective-permute-done | bytes 221216 | tf_op jit(solution)/shard_map/ppermute | solution.py:33
  28.4 1.2 collective-permute-done.4.refs_5_
  29.6 7.3 %collective-permute-done.6.refs_7_ = bf16[72,1536]{1,0:T(8,128)(2,1)S(1)} collective-permute-done((bf16[72,1536]{1,0:T(8,128)(2,1)S(1)}, bf16[72,1536]{1,0:T(8,128)(2,1)S(1)}, u32[]{:S(2)}, u32[]{:S(2)}) %collective-permute-start.6) | collective-permute-done | bytes 221216 | tf_op jit(solution)/shard_map/ppermute | solution.py:33
  36.9 4.3 %qkv.1 = (bf16[8,72,256]{2,1,0:T(8,128)(2,1)S(1)}, bf16[8,72,384]{2,1,0:T(8,128)(2,1)S(1)}) custom-call(s32[3]{0:T(128)S(1)} %pad_add_fusion.place, s32[8]{0:T(128)S(1)} %copy-done.6, f32[8,5,1536]{2,1,0:T(8,128)S(1)} %copy.64.mod, bf16[256,256]{1,0:T(8,128)(2,1)S(1)} %fusion.1.perm, bf16[1536,640]{1,0:T(8,128)(2,1)S(1)} %arrange.1.weight, ...), custom_call_target="tpu_custom_call" | custom-call | flops 1132462080 | bytes 4500000 | tf_op jit(solution)/shard_map/qkv/pallas_call | solution.py:109
  43.2 1.7 collective-permute-start.10
  44.9 2.8 %collective-permute-start.11 = (bf16[96,1536]{1,0:T(8,128)(2,1)S(1)}, bf16[96,1536]{1,0:T(8,128)(2,1)S(1)}, u32[]{:S(2)}, u32[]{:S(2)}) collective-permute-start(bf16[96,1536]{1,0:T(8,128)(2,1)S(1)} %constant_dynamic-slice_fusion), channel_id=1, source_target_pairs={{0,128},{32,160},{64,192},{96,224},{128,0},{160,32},{192,64},{224,... | collective-permute-start | bytes 884744 | tf_op jit(solution)/shard_map/ppermute | solution.py:33
  48.5 4.5 %collective-permute-done.8 = bf16[96,1536]{1,0:T(8,128)(2,1)S(1)} collective-permute-done((bf16[96,1536]{1,0:T(8,128)(2,1)S(1)}, bf16[96,1536]{1,0:T(8,128)(2,1)S(1)}, u32[]{:S(2)}, u32[]{:S(2)}) %collective-permute-start.8) | collective-permute-done | bytes 294944 | tf_op jit(solution)/shard_map/ppermute | solution.py:33
  53.1 18.2 %collective-permute-start.14 = (bf16[96,1536]{1,0:T(8,128)(2,1)S(1)}, bf16[96,1536]{1,0:T(8,128)(2,1)S(1)}, u32[]{:S(2)}, u32[]{:S(2)}) collective-permute-start(bf16[96,1536]{1,0:T(8,128)(2,1)S(1)} %constant_dynamic-slice_fusion), channel_id=1, source_target_pairs={{0,224},{32,0},{64,32},{96,64},{128,96},{160,128},{192,160},{224,1... | collective-permute-start | bytes 884744 | tf_op jit(solution)/shard_map/ppermute | solution.py:33
  71.5 7.1 %collective-permute-done.14 = bf16[96,1536]{1,0:T(8,128)(2,1)S(1)} collective-permute-done((bf16[96,1536]{1,0:T(8,128)(2,1)S(1)}, bf16[96,1536]{1,0:T(8,128)(2,1)S(1)}, u32[]{:S(2)}, u32[]{:S(2)}) %collective-permute-start.14) | collective-permute-done | bytes 294944 | tf_op jit(solution)/shard_map/ppermute | solution.py:33
  78.7 1.8 %collective-permute-start.15 = (bf16[8,96,1536]{2,1,0:T(8,128)(2,1)S(1)}, bf16[8,96,1536]{2,1,0:T(8,128)(2,1)}, u32[]{:S(2)}, u32[]{:S(2)}) collective-permute-start(bf16[8,96,1536]{2,1,0:T(8,128)(2,1)S(1)} %bitcast_dynamic-update-slice_fusion.near), channel_id=1, source_target_pairs={{0,1},{1,0},{2,3},{3,2},{4,5},{5,4},{6,7},{7,6},{8,9},{9,8},{10,11... | collective-permute-start | bytes 7077896 | tf_op jit(solution)/shard_map/ppermute | solution.py:33
  80.5 3.1 %collective-permute-start.7 = (bf16[8,72,256]{2,1,0:T(8,128)(2,1)S(1)}, bf16[8,72,256]{2,1,0:T(8,128)(2,1)S(1)}, u32[]{:S(2)}, u32[]{:S(2)}) collective-permute-start(bf16[8,72,256]{2,1,0:T(8,128)(2,1)S(1)} %copy-done.10), channel_id=1, source_target_pairs={{0,2},{2,0},{1,3},{3,1},{4,6},{6,4},{5,7},{7,5},{8,10},{10,8},{9,1... | collective-permute-start | bytes 884744 | tf_op jit(solution)/shard_map/ppermute | solution.py:33
  83.6 7.1 %collective-permute-done.7.qb = bf16[8,72,256]{2,1,0:T(8,128)(2,1)S(1)} collective-permute-done((bf16[8,72,256]{2,1,0:T(8,128)(2,1)S(1)}, bf16[8,72,256]{2,1,0:T(8,128)(2,1)S(1)}, u32[]{:S(2)}, u32[]{:S(2)}) %collective-permute-start.7) | collective-permute-done | bytes 294944 | tf_op jit(solution)/shard_map/ppermute | solution.py:33
  91.4 3.0 %all-gather.3.cloned.1.call-done = bf16[128,72,384]{2,1,0:T(8,128)(2,1)} async-done(((bf16[8,72,384]{2,1,0:T(8,128)(2,1)}), bf16[128,72,384]{2,1,0:T(8,128)(2,1)}) %all-gather.3.cloned.1.call-update) | async-done | bytes 7077904 | tf_op jit(solution)/shard_map/all_gather | solution.py:362
  94.5 1.0 copy-done.11
  95.5 1.0 copy-done.13
  96.4 30.6 %attend.1 = bf16[8,2,72,256]{3,2,1,0:T(8,128)(2,1)S(1)} custom-call(s32[3]{0:T(128)S(1)} %pad_add_fusion.place, s32[8,8]{1,0:T(8,128)S(1)} %copy-done.14, bf16[8,72,256]{2,1,0:T(8,128)(2,1)S(1)} %copy-done.11, bf16[8,72,256]{2,1,0:T(8,128)(2,1)S(1)} %copy-done.13, bf16[16,8,72,384]{3,2,1,0:T(8,128)(2,1)} %bitcast.43), custom_call_target="tpu_custom_call" | custom-call | flops 8000000000 | bytes 8000000 | tf_op jit(solution)/shard_map/attend/pallas_call | solution.py:240
  127.9 6.6 %all-to-all-start = ((bf16[16,72,256]{2,1,0:T(8,128)(2,1)}), bf16[16,72,256]{2,1,0:T(8,128)(2,1)}, u32[]{:S(2)}, u32[]{:S(2)}) async-start(bf16[16,72,256]{2,1,0:T(8,128)(2,1)} %bitcast.39), calls=%async_computation | async-start | bytes 1179648 | tf_op jit(solution)/shard_map/all_to_all | solution.py:371
  135.4 10.7 %all-to-all-done.parts = bf16[16,72,256]{2,1,0:T(8,128)(2,1)} async-done(((bf16[16,72,256]{2,1,0:T(8,128)(2,1)}), bf16[16,72,256]{2,1,0:T(8,128)(2,1)}, u32[]{:S(2)}, u32[]{:S(2)}) %all-to-all-start) | async-done | bytes 589856 | tf_op jit(solution)/shard_map/all_to_all | solution.py:371
  146.2 1.0 copy-done.1
  148.1 5.1 %finish.1 = (bf16[72,1536]{1,0:T(8,128)(2,1)}, bf16[72,64]{1,0:T(8,128)(2,1)S(1)}) custom-call(s32[3]{0:T(128)S(1)} %pad_add_fusion.place, s32[8]{0:T(128)S(1)} %copy-done.6, bf16[16,72,256]{2,1,0:T(8,128)(2,1)} %all-to-all-done.parts, bf16[8,96,1536]{2,1,0:T(8,128)(2,1)S(1)} %bitcast_dynamic-update-slice_fusion.near, ...), custom_call_target="tpu_custom_call" | custom-call | flops 339738624 | bytes 6000000 | tf_op jit(solution)/shard_map/finish/pallas_call | solution.py:321
  153.3 8.6 %all_to_all.10 = bf16[8,72,64]{1,2,0:T(8,128)(2,1)S(1)} all-to-all(bf16[8,72,64]{1,2,0:T(8,128)(2,1)S(1)} %broadcast_in_dim.8), channel_id=1, replica_groups=mesh['x'=4,'ylo'=2,'z'=8,'yhi'=2,'core'=2] {'x','ylo'}, dimensions={0} | all-to-all | bytes 147456 | tf_op jit(solution)/shard_map/all_to_all | solution.py:386
  162.3 4.6 %collective-permute-start.17 = (bf16[5,1,48,16]{2,3,1,0:T(8,128)(2,1)S(1)}, bf16[5,1,48,16]{2,3,1,0:T(8,128)(2,1)S(1)}, u32[]{:S(2)}, u32[]{:S(2)}) collective-permute-start(bf16[5,1,48,16]{2,3,1,0:T(8,128)(2,1)S(1)} %get-tuple-element.23), channel_id=1, source_target_pairs={{1,0},{2,1},{3,2},{4,3},{5,4},{6,5},{7,6},{8,7},{9,8},{10,9},{11,1... | collective-permute-start | bytes 23048 | tf_op jit(solution)/shard_map/ppermute | solution.py:393
  166.9 3.5 %collective-permute-start.16 = (bf16[5,1,48,16]{2,3,1,0:T(8,128)(2,1)S(1)}, bf16[5,1,48,16]{2,3,1,0:T(8,128)(2,1)S(1)}, u32[]{:S(2)}, u32[]{:S(2)}) collective-permute-start(bf16[5,1,48,16]{2,3,1,0:T(8,128)(2,1)S(1)} %get-tuple-element.22), channel_id=1, source_target_pairs={{0,1},{1,2},{2,3},{3,4},{4,5},{5,6},{6,7},{7,8},{8,9},{9,10},{10,1... | collective-permute-start | bytes 23048 | tf_op jit(solution)/shard_map/ppermute | solution.py:392
  (106 shorter events, 10.8 us)
Async XLA Ops:
  7.2 35.6 %copy-start = (bf16[192,1536]{1,0:T(8,128)(2,1)S(1)}, bf16[192,1536]{1,0:T(8,128)(2,1)}, u32[]{:S(2)}) copy-start(bf16[192,1536]{1,0:T(8,128)(2,1)} %param.16) | copy-start | bytes 1769476
  7.2 87.3 %all-gather.3.cloned.1.call-start = ((), (), s32[]{:S(2)}) async-start(), calls=%async_computation.2 | async-start | bytes 7520256 | tf_op jit(solution)/shard_map/all_gather | solution.py:362
  7.2 14.5 %collective-permute-start = (bf16[72,1536]{1,0:T(8,128)(2,1)}, bf16[72,1536]{1,0:T(8,128)(2,1)S(1)}, u32[]{:S(2)}, u32[]{:S(2)}) collective-permute-start(bf16[72,1536]{1,0:T(8,128)(2,1)} %bitcast.30), channel_id=1, source_target_pairs={{0,32},{32,64},{64,96},{96,128},{128,160},{160,192},{192,224},{224... | collective-permute-start | bytes 663560 | tf_op jit(solution)/shard_map/ppermute | solution.py:33
  9.4 13.5 %collective-permute-start.1 = (bf16[72,1536]{1,0:T(8,128)(2,1)}, bf16[72,1536]{1,0:T(8,128)(2,1)}, u32[]{:S(2)}, u32[]{:S(2)}) collective-permute-start(bf16[72,1536]{1,0:T(8,128)(2,1)} %bitcast.31), channel_id=1, source_target_pairs={{0,64},{32,96},{64,128},{96,160},{128,192},{160,224},{192,0},{224,... | collective-permute-start | bytes 663560 | tf_op jit(solution)/shard_map/ppermute | solution.py:33
  10.6 17.8 %collective-permute-start.2 = (bf16[72,1536]{1,0:T(8,128)(2,1)}, bf16[72,1536]{1,0:T(8,128)(2,1)}, u32[]{:S(2)}, u32[]{:S(2)}) collective-permute-start(bf16[72,1536]{1,0:T(8,128)(2,1)} %bitcast.32), channel_id=1, source_target_pairs={{0,96},{32,128},{64,160},{96,192},{128,224},{160,0},{192,32},{224,... | collective-permute-start | bytes 663560 | tf_op jit(solution)/shard_map/ppermute | solution.py:33
  12.4 16.1 %collective-permute-start.3 = (bf16[72,1536]{1,0:T(8,128)(2,1)}, bf16[72,1536]{1,0:T(8,128)(2,1)}, u32[]{:S(2)}, u32[]{:S(2)}) collective-permute-start(bf16[72,1536]{1,0:T(8,128)(2,1)} %bitcast.33), channel_id=1, source_target_pairs={{0,128},{32,160},{64,192},{96,224},{128,0},{160,32},{192,64},{224,... | collective-permute-start | bytes 663560 | tf_op jit(solution)/shard_map/ppermute | solution.py:33
  14.1 15.5 %collective-permute-start.4 = (bf16[72,1536]{1,0:T(8,128)(2,1)}, bf16[72,1536]{1,0:T(8,128)(2,1)}, u32[]{:S(2)}, u32[]{:S(2)}) collective-permute-start(bf16[72,1536]{1,0:T(8,128)(2,1)} %bitcast.34), channel_id=1, source_target_pairs={{0,160},{32,192},{64,224},{96,0},{128,32},{160,64},{192,96},{224,1... | collective-permute-start | bytes 663560 | tf_op jit(solution)/shard_map/ppermute | solution.py:33
  18.1 1.5 copy-start.8
  19.5 2.2 %copy-start.2 = (bf16[1,72,1536]{2,1,0:T(8,128)(2,1)S(1)}, bf16[1,72,1536]{2,1,0:T(8,128)(2,1)}, u32[]{:S(2)}) copy-start(bf16[1,72,1536]{2,1,0:T(8,128)(2,1)} %param.11) | copy-start | bytes 663556
  19.5 17.4 %copy-start.6 = (s32[8]{0:T(128)S(1)}, s32[8]{0:T(128)}, u32[]{:S(2)}) copy-start(s32[8]{0:T(128)} %levels.3) | copy-start | bytes 100
  21.7 7.9 %collective-permute-start.5 = (bf16[72,1536]{1,0:T(8,128)(2,1)S(1)}, bf16[72,1536]{1,0:T(8,128)(2,1)S(1)}, u32[]{:S(2)}, u32[]{:S(2)}) collective-permute-start(bf16[72,1536]{1,0:T(8,128)(2,1)S(1)} %bitcast.35), channel_id=1, source_target_pairs={{0,192},{32,224},{64,0},{96,32},{128,64},{160,96},{192,128},{224,1... | collective-permute-start | bytes 663560 | tf_op jit(solution)/shard_map/ppermute | solution.py:33
  23.0 13.9 %collective-permute-start.6 = (bf16[72,1536]{1,0:T(8,128)(2,1)S(1)}, bf16[72,1536]{1,0:T(8,128)(2,1)S(1)}, u32[]{:S(2)}, u32[]{:S(2)}) collective-permute-start(bf16[72,1536]{1,0:T(8,128)(2,1)S(1)} %bitcast.36), channel_id=1, source_target_pairs={{0,224},{32,0},{64,32},{96,64},{128,96},{160,128},{192,160},{224,1... | collective-permute-start | bytes 663560 | tf_op jit(solution)/shard_map/ppermute | solution.py:33
  42.8 37.7 %copy-start.10 = (bf16[8,72,256]{2,1,0:T(8,128)(2,1)S(1)}, bf16[8,72,256]{2,1,0:T(8,128)(2,1)}, u32[]{:S(2)}) copy-start(bf16[8,72,256]{2,1,0:T(8,128)(2,1)} %copy-done.9) | copy-start | bytes 884740
  42.8 51.7 %copy-start.14 = (s32[8,8]{1,0:T(8,128)S(1)}, s32[8,8]{1,0:T(8,128)}, u32[]{:S(2)}) copy-start(s32[8,8]{1,0:T(8,128)} %mask.1) | copy-start | bytes 772
  42.8 10.3 %collective-permute-start.8 = (bf16[96,1536]{1,0:T(8,128)(2,1)S(1)}, bf16[96,1536]{1,0:T(8,128)(2,1)S(1)}, u32[]{:S(2)}, u32[]{:S(2)}) collective-permute-start(bf16[96,1536]{1,0:T(8,128)(2,1)S(1)} %constant_dynamic-slice_fusion), channel_id=1, source_target_pairs={{0,32},{32,64},{64,96},{96,128},{128,160},{160,192},{192,224},{224... | collective-permute-start | bytes 884744 | tf_op jit(solution)/shard_map/ppermute | solution.py:33
  43.1 10.0 %collective-permute-start.9 = (bf16[96,1536]{1,0:T(8,128)(2,1)S(1)}, bf16[96,1536]{1,0:T(8,128)(2,1)S(1)}, u32[]{:S(2)}, u32[]{:S(2)}) collective-permute-start(bf16[96,1536]{1,0:T(8,128)(2,1)S(1)} %constant_dynamic-slice_fusion), channel_id=1, source_target_pairs={{0,64},{32,96},{64,128},{96,160},{128,192},{160,224},{192,0},{224,... | collective-permute-start | bytes 884744 | tf_op jit(solution)/shard_map/ppermute | solution.py:33
  43.2 28.2 %collective-permute-start.10 = (bf16[96,1536]{1,0:T(8,128)(2,1)S(1)}, bf16[96,1536]{1,0:T(8,128)(2,1)S(1)}, u32[]{:S(2)}, u32[]{:S(2)}) collective-permute-start(bf16[96,1536]{1,0:T(8,128)(2,1)S(1)} %constant_dynamic-slice_fusion), channel_id=1, source_target_pairs={{0,96},{32,128},{64,160},{96,192},{128,224},{160,0},{192,32},{224,... | collective-permute-start | bytes 884744 | tf_op jit(solution)/shard_map/ppermute | solution.py:33
  44.9 26.5 %collective-permute-start.11 = (bf16[96,1536]{1,0:T(8,128)(2,1)S(1)}, bf16[96,1536]{1,0:T(8,128)(2,1)S(1)}, u32[]{:S(2)}, u32[]{:S(2)}) collective-permute-start(bf16[96,1536]{1,0:T(8,128)(2,1)S(1)} %constant_dynamic-slice_fusion), channel_id=1, source_target_pairs={{0,128},{32,160},{64,192},{96,224},{128,0},{160,32},{192,64},{224,... | collective-permute-start | bytes 884744 | tf_op jit(solution)/shard_map/ppermute | solution.py:33
  47.6 23.8 %collective-permute-start.12 = (bf16[96,1536]{1,0:T(8,128)(2,1)S(1)}, bf16[96,1536]{1,0:T(8,128)(2,1)S(1)}, u32[]{:S(2)}, u32[]{:S(2)}) collective-permute-start(bf16[96,1536]{1,0:T(8,128)(2,1)S(1)} %constant_dynamic-slice_fusion), channel_id=1, source_target_pairs={{0,160},{32,192},{64,224},{96,0},{128,32},{160,64},{192,96},{224,1... | collective-permute-start | bytes 884744 | tf_op jit(solution)/shard_map/ppermute | solution.py:33
  53.1 18.4 %collective-permute-start.13 = (bf16[96,1536]{1,0:T(8,128)(2,1)S(1)}, bf16[96,1536]{1,0:T(8,128)(2,1)S(1)}, u32[]{:S(2)}, u32[]{:S(2)}) collective-permute-start(bf16[96,1536]{1,0:T(8,128)(2,1)S(1)} %constant_dynamic-slice_fusion), channel_id=1, source_target_pairs={{0,192},{32,224},{64,0},{96,32},{128,64},{160,96},{192,128},{224,1... | collective-permute-start | bytes 884744 | tf_op jit(solution)/shard_map/ppermute | solution.py:33
  53.1 25.5 %collective-permute-start.14 = (bf16[96,1536]{1,0:T(8,128)(2,1)S(1)}, bf16[96,1536]{1,0:T(8,128)(2,1)S(1)}, u32[]{:S(2)}, u32[]{:S(2)}) collective-permute-start(bf16[96,1536]{1,0:T(8,128)(2,1)S(1)} %constant_dynamic-slice_fusion), channel_id=1, source_target_pairs={{0,224},{32,0},{64,32},{96,64},{128,96},{160,128},{192,160},{224,1... | collective-permute-start | bytes 884744 | tf_op jit(solution)/shard_map/ppermute | solution.py:33
  78.7 56.8 %collective-permute-start.15 = (bf16[8,96,1536]{2,1,0:T(8,128)(2,1)S(1)}, bf16[8,96,1536]{2,1,0:T(8,128)(2,1)}, u32[]{:S(2)}, u32[]{:S(2)}) collective-permute-start(bf16[8,96,1536]{2,1,0:T(8,128)(2,1)S(1)} %bitcast_dynamic-update-slice_fusion.near), channel_id=1, source_target_pairs={{0,1},{1,0},{2,3},{3,2},{4,5},{5,4},{6,7},{7,6},{8,9},{9,8},{10,11... | collective-permute-start | bytes 7077896 | tf_op jit(solution)/shard_map/ppermute | solution.py:33
  80.5 10.2 %collective-permute-start.7 = (bf16[8,72,256]{2,1,0:T(8,128)(2,1)S(1)}, bf16[8,72,256]{2,1,0:T(8,128)(2,1)S(1)}, u32[]{:S(2)}, u32[]{:S(2)}) collective-permute-start(bf16[8,72,256]{2,1,0:T(8,128)(2,1)S(1)} %copy-done.10), channel_id=1, source_target_pairs={{0,2},{2,0},{1,3},{3,1},{4,6},{6,4},{5,7},{7,5},{8,10},{10,8},{9,1... | collective-permute-start | bytes 884744 | tf_op jit(solution)/shard_map/ppermute | solution.py:33
  96.4 38.1 %copy-start.16 = (bf16[768,128]{1,0:T(8,128)(2,1)S(1)}, bf16[768,128]{1,0:T(8,128)(2,1)}, u32[]{:S(2)}) copy-start(bf16[768,128]{1,0:T(8,128)(2,1)} %param.17) | copy-start | bytes 589828
  96.4 49.8 %copy-start.7 = (f32[64]{0:T(128)S(1)}, f32[64]{0:T(128)}, u32[]{:S(2)}) copy-start(f32[64]{0:T(128)} %param.18) | copy-start | bytes 772
  127.9 18.3 %all-to-all-start = ((bf16[16,72,256]{2,1,0:T(8,128)(2,1)}), bf16[16,72,256]{2,1,0:T(8,128)(2,1)}, u32[]{:S(2)}, u32[]{:S(2)}) async-start(bf16[16,72,256]{2,1,0:T(8,128)(2,1)} %bitcast.39), calls=%async_computation | async-start | bytes 1179648 | tf_op jit(solution)/shard_map/all_to_all | solution.py:371
  146.2 1.0 copy-start.1
  148.1 14.2 %copy-start.17 = (bf16[2,2,48,16]{2,3,1,0:T(8,128)(2,1)S(1)}, bf16[2,2,48,16]{2,3,1,0:T(8,128)(2,1)}, u32[]{:S(2)}) copy-start(bf16[2,2,48,16]{2,3,1,0:T(8,128)(2,1)} %param.19) | copy-start | bytes 18436
  153.2 20.3 %copy-start.15 = (bf16[432,384]{1,0:T(8,128)(2,1)S(1)}, bf16[432,384]{1,0:T(8,128)(2,1)}, u32[]{:S(2)}) copy-start(bf16[432,384]{1,0:T(8,128)(2,1)} %param.20) | copy-start | bytes 995332
  153.2 20.3 %copy-start.18 = (f32[384]{0:T(512)S(1)}, f32[384]{0:T(512)}, u32[]{:S(2)}) copy-start(f32[384]{0:T(512)} %param.21) | copy-start | bytes 4612
  162.3 8.1 %collective-permute-start.17 = (bf16[5,1,48,16]{2,3,1,0:T(8,128)(2,1)S(1)}, bf16[5,1,48,16]{2,3,1,0:T(8,128)(2,1)S(1)}, u32[]{:S(2)}, u32[]{:S(2)}) collective-permute-start(bf16[5,1,48,16]{2,3,1,0:T(8,128)(2,1)S(1)} %get-tuple-element.23), channel_id=1, source_target_pairs={{1,0},{2,1},{3,2},{4,3},{5,4},{6,5},{7,6},{8,7},{9,8},{10,9},{11,1... | collective-permute-start | bytes 23048 | tf_op jit(solution)/shard_map/ppermute | solution.py:393
  166.9 4.4 %collective-permute-start.16 = (bf16[5,1,48,16]{2,3,1,0:T(8,128)(2,1)S(1)}, bf16[5,1,48,16]{2,3,1,0:T(8,128)(2,1)S(1)}, u32[]{:S(2)}, u32[]{:S(2)}) collective-permute-start(bf16[5,1,48,16]{2,3,1,0:T(8,128)(2,1)S(1)} %get-tuple-element.22), channel_id=1, source_target_pairs={{0,1},{1,2},{2,3},{3,4},{4,5},{5,6},{6,7},{7,8},{8,9},{9,10},{10,1... | collective-permute-start | bytes 23048 | tf_op jit(solution)/shard_map/ppermute | solution.py:392
  (7 other events, 5.9 us)
Sparse Core Ops, SparseCore 0:
  42.9 51.5 all-gather.2

commit v2 on v1

--- a/solution.py
+++ b/solution.py
@@ -24,6 +24,7 @@
 SPAN = ("x", "ylo")
 TILE = ("z", "yhi", "core")
 VMEM_LIMIT = 48 * 1024 * 1024
+OFFSETS = ((0, 0), (0, 1), (3, 0), (1, 0), (3, 1), (1, 1), (2, 0), (2, 1))
 
 bf16 = jnp.bfloat16
 f32 = jnp.float32
@@ -41,10 +42,10 @@
 
 def qkv_kernel(place, levels, mod, perm, weight, *refs):
     tokens = refs[:SPANS]
-    q_ref, kv_ref, normed = refs[SPANS:]
+    q_ref, kv_ref, first_ref, normed = refs[SPANS:]
     me = place[0]
     for step in range(SPANS):
-        span = lax.rem(me - step + SPANS, SPANS)
+        span = lax.rem(me // 2 + OFFSETS[step][0], 4) * 2 + lax.rem(me + OFFSETS[step][1], 2)
         level = levels[span]
         values = normalise(tokens[step][...].astype(f32))
         values = values * (1.0 + mod[level, 1:2, :]) + mod[level, 0:1, :]
@@ -57,10 +58,14 @@
             part, weight[block * 256 : (block + 1) * 256, :], preferred_element_type=f32
         )
     for step in range(SPANS):
-        span = lax.rem(me - step + SPANS, SPANS)
+        span = lax.rem(me // 2 + OFFSETS[step][0], 4) * 2 + lax.rem(me + OFFSETS[step][1], 2)
         rows = total[step * ROWS : (step + 1) * ROWS, :].astype(bf16)
         q_ref[span] = rows[:, :LANES] * jnp.asarray(HDIM**-0.5, bf16)
         kv_ref[span] = rows[:, LANES:]
+
+        @pl.when(span == 0)
+        def _():
+            first_ref[...] = tokens[step][...]
 
 
 def arrange_kernel(raw, out):
@@ -111,9 +116,10 @@
         out_shape=(
             jax.ShapeDtypeStruct((SPANS, ROWS, LANES), bf16),
             jax.ShapeDtypeStruct((SPANS, ROWS, KVW), bf16),
+            jax.ShapeDtypeStruct((ROWS, D), bf16),
         ),
         in_specs=[smem, smem] + [vmem] * (3 + SPANS),
-        out_specs=(vmem, vmem),
+        out_specs=(vmem,) * 3,
         scratch_shapes=[pltpu.VMEM((SPANS * ROWS, D), f32)],
         compiler_params=pltpu.CompilerParams(vmem_limit_bytes=VMEM_LIMIT),
         cost_estimate=pl.CostEstimate(
@@ -130,6 +136,63 @@
         parts.append(part)
         value = value - part
     return parts
+
+
+def pack(heads, tops):
+    lane = lax.broadcasted_iota(jnp.int32, (1, LANES), 1)
+    merged = jnp.where(lane < HDIM, heads[0], jnp.where(lane < 2 * HDIM, heads[1], heads[2]))
+    columns = []
+    for head in range(GROUP):
+        columns += split_bf16(tops[head], 3)
+        columns += split_bf16(heads[head][:, 192:193], 2)
+    for index, column in enumerate(columns):
+        merged = jnp.where(lane == 192 + index, column, merged)
+    return merged
+
+
+def attend_first_kernel(place, qa, qb, kv, out):
+    lane = lax.broadcasted_iota(jnp.int32, (1, LANES), 1)
+    rows = 2 * ROWS
+    both = jnp.concatenate([qa[0].astype(f32), qb[0].astype(f32)], axis=0)
+    block = kv[:, 0].astype(f32).reshape(kv.shape[0] * ROWS, KVW)
+    values = jnp.where(lane // HDIM == 3, 1.0, block[:, :LANES]).astype(bf16)
+    keys = block[:, KVW - LANES :].astype(bf16)
+    heads, tops = [], []
+    for head in range(GROUP):
+        query = jnp.where(lane // HDIM == head + 1, both, 0.0).astype(bf16)
+        scores = lax.dot_general(
+            query, keys, (((1,), (1,)), ((), ())), preferred_element_type=f32
+        )
+        top = jnp.max(scores, axis=1, keepdims=True)
+        probs = jnp.exp(scores - top).astype(bf16)
+        heads.append(jnp.dot(probs, values, preferred_element_type=f32))
+        tops.append(top)
+    merged = pack(heads, tops)
+    mine = place[1]
+    for span in range(SPANS):
+        out[span, mine] = merged[:ROWS].astype(bf16)
+        out[span, 1 - mine] = merged[ROWS:].astype(bf16)
+
+
+def attend_first(place, qa, qb, kv):
+    head = pl.BlockSpec((1, ROWS, LANES), lambda i: (0, 0, 0))
+    return pl.pallas_call(
+        attend_first_kernel,
+        grid=(1,),
+        out_shape=jax.ShapeDtypeStruct((SPANS, 2, ROWS, LANES), bf16),
+        in_specs=[
+            pl.BlockSpec(memory_space=pltpu.SMEM),
+            head,
+            head,
+            pl.BlockSpec((kv.shape[0], 1, ROWS, KVW), lambda i: (0, 0, 0, 0)),
+        ],
+        out_specs=pl.BlockSpec((SPANS, 2, ROWS, LANES), lambda i: (0, 0, 0, 0)),
+        compiler_params=pltpu.CompilerParams(vmem_limit_bytes=VMEM_LIMIT),
+        cost_estimate=pl.CostEstimate(
+            flops=600000000, bytes_accessed=2000000, transcendentals=500000
+        ),
+        name="attend_first",
+    )(place, qa, qb, kv)
 
 
 def attend_kernel(
@@ -220,13 +283,8 @@
         mine = place[1]
         for span in range(SPANS):
             heads = [acc[span, head * rows : (head + 1) * rows, :] for head in range(GROUP)]
-            merged = jnp.where(lane < HDIM, heads[0], jnp.where(lane < 2 * HDIM, heads[1], heads[2]))
-            columns = []
-            for head in range(GROUP):
-                columns += split_bf16(peak[span, head * rows : (head + 1) * rows, 0:1], 3)
-                columns += split_bf16(heads[head][:, 192:193], 2)
-            for index, column in enumerate(columns):
-                merged = jnp.where(lane == 192 + index, column, merged)
+            tops = [peak[span, head * rows : (head + 1) * rows, 0:1] for head in range(GROUP)]
+            merged = pack(heads, tops)
             out[span, mine] = merged[:ROWS].astype(bf16)
             out[span, 1 - mine] = merged[ROWS:].astype(bf16)
 
@@ -273,9 +331,7 @@
     )(place, mask, qa, qb, kv)
 
 
-def finish_kernel(
-    place, levels, parts, near, far, tokens, mod, head_full, bias, hidden, patches, weight
-):
+def finish_kernel(place, levels, parts, near, far, tokens, mod, *refs, decode):
     lane = lax.broadcasted_iota(jnp.int32, (HDIM, LANES), 1)
     slot = lax.broadcasted_iota(jnp.int32, (HDIM, LANES), 0)
     head = lane // HDIM
@@ -283,12 +339,16 @@
     sums = jnp.where((slot >= head * 5 + 3) & (slot < head * 5 + 5) & (head < 3), 1.0, 0.0).astype(
         bf16
     )
+    if decode:
+        head_full, bias, patches, weight = refs
+    else:
+        hidden, weight = refs
     total = jnp.zeros((ROWS, D), f32)
     core = place[2]
     for step in range(SPANS):
         group = lax.rem(place[0] - step + SPANS, SPANS)
-        weight[:96, :] = jnp.where(core == 0, near[step], far[step])
-        weight[96:, :] = jnp.where(core == 0, far[step], near[step])
+        weight[step, :96, :] = jnp.where(core == 0, near[step], far[step])
+        weight[step, 96:, :] = jnp.where(core == 0, far[step], near[step])
         tops, totals, outs = [], [], []
         for half in range(2):
             part = parts[group * 2 + half]
@@ -301,38 +361,35 @@
             totals[0] * scale[0] + totals[1] * scale[1]
         )
         total += jnp.dot(
-            blended[:, :192].astype(bf16),
-            weight[...],
-            preferred_element_type=f32,
-        )
-    level = levels[place[0]]
+            blended[:, :192].astype(bf16), weight[step], preferred_element_type=f32
+        )
+    level = levels[0] if decode else levels[place[0]]
     result = (tokens[...].astype(f32) + mod[level, 2:3, :] * total).astype(bf16)
-    hidden[...] = result
-    first = levels[0]
-    shaped = normalise(result.astype(f32)) * (1.0 + mod[first, 4:5, :]) + mod[first, 3:4, :]
-    patches[...] = (
-        jnp.dot(shaped.astype(bf16), head_full[...], preferred_element_type=f32) + bias[...]
-    ).astype(bf16)
-
-
-def finish(place, levels, parts, near, far, tokens, modulation, head_full, bias):
+    if decode:
+        shaped = normalise(result.astype(f32)) * (1.0 + mod[level, 4:5, :]) + mod[level, 3:4, :]
+        patches[...] = (
+            jnp.dot(shaped.astype(bf16), head_full[...], preferred_element_type=f32) + bias[...]
+        ).astype(bf16)
+    else:
+        hidden[...] = result
+
+
+def finish(place, levels, parts, near, far, tokens, modulation, *extra):
     smem = pl.BlockSpec(memory_space=pltpu.SMEM)
     vmem = pl.BlockSpec(memory_space=pltpu.VMEM)
+    decode = len(extra) > 0
     return pl.pallas_call(
-        finish_kernel,
-        out_shape=(
-            jax.ShapeDtypeStruct((ROWS, D), bf16),
-            jax.ShapeDtypeStruct((ROWS, 4 * LCH), bf16),
-        ),
-        in_specs=[smem, smem] + [vmem] * 7,
-        out_specs=(vmem, vmem),
-        scratch_shapes=[pltpu.VMEM((192, D), bf16)],
+        functools.partial(finish_kernel, decode=decode),
+        out_shape=jax.ShapeDtypeStruct((ROWS, 4 * LCH if decode else D), bf16),
+        in_specs=[smem, smem] + [vmem] * (5 + len(extra)),
+        out_specs=vmem,
+        scratch_shapes=[pltpu.VMEM((SPANS, 192, D), bf16)],
         compiler_params=pltpu.CompilerParams(vmem_limit_bytes=VMEM_LIMIT),
         cost_estimate=pl.CostEstimate(
             flops=2 * ROWS * D * D, bytes_accessed=6000000, transcendentals=0
         ),
-        name="finish",
-    )(place, levels, parts, near, far, tokens, modulation, head_full, bias)
+        name="finish_first" if decode else "finish",
+    )(place, levels, parts, near, far, tokens, modulation, *extra)
 
 
 def per_device(
@@ -354,37 +411,44 @@
     place = jnp.stack([span, yhi, core]).astype(jnp.int32)
     own = tokens[0]
 
-    blocks = [own] + [shift(own, SPAN, SPANS, step) for step in range(1, SPANS)]
+    beside = shift(own, "ylo", 2, 1)
+    lower, upper = shift(own, "x", 4, 1), shift(own, "x", 4, -1)
+    lower_beside, upper_beside = shift(beside, "x", 4, 1), shift(beside, "x", 4, -1)
+    across, across_beside = shift(lower, "x", 4, 1), shift(upper_beside, "x", 4, -1)
+    blocks = [own, beside, lower, upper, lower_beside, upper_beside, across, across_beside]
 
     weight = arrange(qkv_weight)
-    q_own, kv_own = project_spans(place, noise_steps, modulation, weight, blocks)
+    q_own, kv_own, first = project_spans(place, noise_steps, modulation, weight, blocks)
 
     kv = lax.all_gather(kv_own, ("z", "core"))
     q_other = shift(q_own, "yhi", 2, 1)
 
     half = lax.dynamic_slice_in_dim(out_weight, core * 96, 96, 0)
     half, _ = lax.optimization_barrier((half, q_own))
-    halves = [half] + [shift(half, SPAN, SPANS, step) for step in range(1, SPANS)]
-    stacked = jnp.stack(halves)
-    other = shift(stacked, "core", 2, 1)
+    near = jnp.stack([half] + [shift(half, SPAN, SPANS, step) for step in range(1, SPANS)])
+    far = shift(near, "core", 2, 1)
+
+    first_partial = attend_first(place, q_own, q_other, kv)
+    first_parts = lax.all_to_all(
+        first_partial.reshape(2 * SPANS, ROWS, LANES), SPAN + ("yhi",), 0, 0
+    )
     partial = attend(place, span_mask, q_own, q_other, kv)
-    parts = lax.all_to_all(
-        partial.reshape(2 * SPANS, ROWS, LANES), SPAN + ("yhi",), 0, 0
-    )
-    hidden, patches = finish(
+    parts = lax.all_to_all(partial.reshape(2 * SPANS, ROWS, LANES), SPAN + ("yhi",), 0, 0)
+    first_parts, _ = lax.optimization_barrier((first_parts, partial))
+    patches = finish(
         place,
         noise_steps,
-        parts,
-        stacked,
-        other,
-        own,
+        first_parts,
+        near,
+        far,
+        first,
         modulation,
         head_weight.reshape(D, 4 * LCH),
         head_bias[None, :],
     )
-
-    spread = lax.all_to_all(jnp.broadcast_to(patches[None], (SPANS,) + patches.shape), SPAN, 0, 0)
-    latent = spread[0].reshape(LF, TCOL, 2, 2, LCH)
+    hidden = finish(place, noise_steps, parts, near, far, own, modulation)
+
+    latent = patches.reshape(LF, TCOL, 2, 2, LCH)
     latent = jnp.transpose(latent, (0, 2, 1, 3, 4)).reshape(LF, 2, 2 * TCOL, LCH)
     frames = jnp.concatenate([frame_cache, latent], axis=0)
     up = [(i, i + 1) for i in range(31)]
@@ -394,14 +458,15 @@
     padded = jnp.concatenate([above, frames, below], axis=1)
     padded = jnp.pad(padded, ((0, 0), (0, 0), (1, 1), (0, 0)))
     mine = lax.dynamic_slice_in_dim(padded, span * 6, 8, axis=2)
-    pieces = []
-    for a in range(3):
-        for b in range(3):
-            for e in range(3):
-                pieces.append(mine[a : a + 3, b : b + 2, e : e + 6])
-    cells = jnp.concatenate(pieces, axis=-1).reshape(36, 27 * LCH)
-    product = jnp.dot(cells, conv_weight, preferred_element_type=f32) + conv_bias
-    decoded = product.astype(bf16).reshape(3, 2, 6, VCH)
+    product = lax.conv_general_dilated(
+        mine[None],
+        conv_weight.reshape(3, 3, 3, LCH, VCH),
+        (1, 1, 1),
+        "VALID",
+        dimension_numbers=("NDHWC", "DHWIO", "NDHWC"),
+        preferred_element_type=f32,
+    )
+    decoded = (product[0] + conv_bias).astype(bf16)
     return (hidden[None], decoded)
 
 

time: 183 us -> 174 us (0.951)
  blocking collectives: 8.62 us -> 0 us
  starting transfers between devices: 54.5 us -> 46.5 us
  Pallas kernels: 42.1 us -> 48.5 us
    ppermute x16, starting transfers between devices: 39.8 us -> 25.3 us  [shift(): lax.ppermute(block, axis, [(i, (i + step) % count) for i in range(count)])]
    ppermute x16, waiting for transfers between devices: 32.7 us -> 44.5 us  [shift(): lax.ppermute(block, axis, [(i, (i + step) % count) for i in range(count)])]
    all_to_all x1, waiting for transfers between devices: 10.7 us -> 0.01 us  [per_device(): lax.all_to_all(partial.reshape(2 * SPANS, ROWS, LANES), SPAN + ('yhi',),...]
    all_to_all x1 -> x0, blocking collectives: 8.62 us -> none  [per_device(): lax.all_to_all(jnp.broadcast_to(patches[None], (SPANS,) + patches.shape),...]
    pallas_call x1 -> x3, Pallas kernels: 5.11 us -> 12.3 us  [the longest x2 9.34 us: finish(): pl.pallas_call(functools.partial(finish_kernel, decode=decode), out_shape...]
    all_to_all x0 -> x1, starting transfers between devices: none -> 6.57 us  [per_device(): lax.all_to_all(first_partial.reshape(2 * SPANS, ROWS, LANES), SPAN + ('yh...]
    ppermute x1, starting transfers between devices: 4.62 us -> 1.92 us  [per_device(): below = lax.ppermute(frames[:, 0:1], TILE, down)]
    ppermute x1, starting transfers between devices: 3.49 us -> 5.98 us  [per_device(): above = lax.ppermute(frames[:, 1:2], TILE, up)]
  transfers between devices with their start and end apart: 20 -> 21, of which waited for: 9 -> 7; matrix products, arithmetic and copies ran while one was open for 1% -> 2% of each run, Pallas kernels for 18% -> 25%
where the time goes in v2:
time: 174 us
  Pallas kernels  48.5 us (28%)
  waiting for transfers between devices  47.1 us (27%)
  starting transfers between devices  46.5 us (27%)
  local copies, waits for them, and re-layouts  14.8 us (9%)
  between operations  14.4 us (8%)
  matrix products  1.92 us (1%)
    ppermute x16, waiting for transfers between devices, shift(): lax.ppermute(block, axis, [(i, (i + step) % count) for i in range(count)])  44.5 us
    pallas_call x1, Pallas kernels, attend(): pl.pallas_call(attend_kernel, grid=(SPANS,), out_shape=jax.ShapeDtypeStru...  29.6 us
    ppermute x16, starting transfers between devices, shift(): lax.ppermute(block, axis, [(i, (i + step) % count) for i in range(count)])  25.3 us
    unnamed x52, local copies, waits for them, and re-layouts  13.2 us
    pallas_call x2, Pallas kernels, finish(): pl.pallas_call(functools.partial(finish_kernel, decode=decode), out_shape...  9.34 us
    all_to_all x1, starting transfers between devices, per_device(): lax.all_to_all(partial.reshape(2 * SPANS, ROWS, LANES), SPAN + ('yhi',),...  6.67 us
    all_to_all x1, starting transfers between devices, per_device(): lax.all_to_all(first_partial.reshape(2 * SPANS, ROWS, LANES), SPAN + ('yh...  6.57 us
    ppermute x1, starting transfers between devices, per_device(): above = lax.ppermute(frames[:, 1:2], TILE, up)  5.98 us
  transfers between devices with their start and end apart: 21, of which 7 were waited for; matrix products, arithmetic and copies ran while one was open for 2% of the time, Pallas kernels for 25%

profile of v2, /device:TPU:1, one launch (start us, length us, event | category | flops | bytes accessed | tf_op | source)
XLA Modules:
  0.0 174.1 jit_solution(16880588036350757347)
XLA Ops:
  7.2 3.4 %collective-permute-start.2 = (bf16[72,1536]{1,0:T(8,128)(2,1)}, bf16[72,1536]{1,0:T(8,128)(2,1)S(1)}, u32[]{:S(2)}, u32[]{:S(2)}) collective-permute-start(bf16[72,1536]{1,0:T(8,128)(2,1)} %bitcast.38), channel_id=1, source_target_pairs={{0,192},{64,0},{128,64},{192,128},{1,193},{65,1},{129,65},{193,129... | collective-permute-start | bytes 663560 | tf_op jit(solution)/shard_map/ppermute | solution.py:34
  10.6 1.3 collective-permute-start
  11.9 1.1 copy.26.mod
  13.0 1.5 copy-done.17
  14.5 2.1 %arrange.1.weight = bf16[1536,640]{1,0:T(8,128)(2,1)S(1)} custom-call(bf16[768,1152]{1,0:T(8,128)(2,1)S(1)} %copy-done.17), custom_call_target="tpu_custom_call" | custom-call | flops 4000000000 | bytes 4000000 | tf_op jit(solution)/shard_map/arrange/pallas_call | solution.py:96
  16.6 2.8 %collective-permute-start.4 = (bf16[72,1536]{1,0:T(8,128)(2,1)S(1)}, bf16[72,1536]{1,0:T(8,128)(2,1)S(1)}, u32[]{:S(2)}, u32[]{:S(2)}) collective-permute-start(bf16[72,1536]{1,0:T(8,128)(2,1)S(1)} %collective-permute-done.refs_1_), channel_id=1, source_target_pairs={{0,192},{64,0},{128,64},{192,128},{1,193},{65,1},{129,65},{193,129... | collective-permute-start | bytes 663560 | tf_op jit(solution)/shard_map/ppermute | solution.py:34
  19.6 2.7 %collective-permute-done.4.refs_5_ = bf16[72,1536]{1,0:T(8,128)(2,1)S(1)} collective-permute-done((bf16[72,1536]{1,0:T(8,128)(2,1)S(1)}, bf16[72,1536]{1,0:T(8,128)(2,1)S(1)}, u32[]{:S(2)}, u32[]{:S(2)}) %collective-permute-start.4) | collective-permute-done | bytes 221216 | tf_op jit(solution)/shard_map/ppermute | solution.py:34
  22.2 3.1 %collective-permute-start.6 = (bf16[72,1536]{1,0:T(8,128)(2,1)S(1)}, bf16[72,1536]{1,0:T(8,128)(2,1)S(1)}, u32[]{:S(2)}, u32[]{:S(2)}) collective-permute-start(bf16[72,1536]{1,0:T(8,128)(2,1)S(1)} %collective-permute-done.4.refs_5_), channel_id=1, source_target_pairs={{0,192},{64,0},{128,64},{192,128},{1,193},{65,1},{129,65},{193,129... | collective-permute-start | bytes 663560 | tf_op jit(solution)/shard_map/ppermute | solution.py:34
  25.4 4.6 %collective-permute-done.5.refs_6_ = bf16[72,1536]{1,0:T(8,128)(2,1)S(1)} collective-permute-done((bf16[72,1536]{1,0:T(8,128)(2,1)S(1)}, bf16[72,1536]{1,0:T(8,128)(2,1)S(1)}, u32[]{:S(2)}, u32[]{:S(2)}) %collective-permute-start.5) | collective-permute-done | bytes 221216 | tf_op jit(solution)/shard_map/ppermute | solution.py:34
  30.0 4.5 %qkv.1 = (bf16[8,72,256]{2,1,0:T(8,128)(2,1)S(1)}, bf16[8,72,384]{2,1,0:T(8,128)(2,1)}, bf16[72,1536]{1,0:T(8,128)(2,1)S(1)}) custom-call(s32[3]{0:T(128)S(1)} %pad_add_fusion.place, s32[8]{0:T(128)S(1)} %copy-done.15, f32[8,5,1536]{2,1,0:T(8,128)S(1)} %copy.26.mod, bf16[256,256]{1,0:T(8,128)(2,1)S(1)} %fusion.perm, bf16[1536,640]{1,0:T(8,128)(2,1)S(1)} %arrange.1.weight, ...), custom_call_target="tpu_custom_call" | custom-call | flops 1132462080 | bytes 4500000 | tf_op jit(solution)/shard_map/qkv/pallas_call | solution.py:114
  36.0 2.2 %collective-permute-start.14 = (bf16[96,1536]{1,0:T(8,128)(2,1)S(1)}, bf16[96,1536]{1,0:T(8,128)(2,1)S(1)}, u32[]{:S(2)}, u32[]{:S(2)}) collective-permute-start(bf16[96,1536]{1,0:T(8,128)(2,1)S(1)} %constant_dynamic-slice_fusion), channel_id=1, source_target_pairs={{0,224},{32,0},{64,32},{96,64},{128,96},{160,128},{192,160},{224,1... | collective-permute-start | bytes 884744 | tf_op jit(solution)/shard_map/ppermute | solution.py:34
  38.2 3.3 %collective-permute-start.11 = (bf16[96,1536]{1,0:T(8,128)(2,1)S(1)}, bf16[96,1536]{1,0:T(8,128)(2,1)S(1)}, u32[]{:S(2)}, u32[]{:S(2)}) collective-permute-start(bf16[96,1536]{1,0:T(8,128)(2,1)S(1)} %constant_dynamic-slice_fusion), channel_id=1, source_target_pairs={{0,128},{32,160},{64,192},{96,224},{128,0},{160,32},{192,64},{224,... | collective-permute-start | bytes 884744 | tf_op jit(solution)/shard_map/ppermute | solution.py:34
  41.5 1.1 collective-permute-start.8
  42.7 14.7 %collective-permute-done.8 = bf16[96,1536]{1,0:T(8,128)(2,1)S(1)} collective-permute-done((bf16[96,1536]{1,0:T(8,128)(2,1)S(1)}, bf16[96,1536]{1,0:T(8,128)(2,1)S(1)}, u32[]{:S(2)}, u32[]{:S(2)}) %collective-permute-start.8) | collective-permute-done | bytes 294944 | tf_op jit(solution)/shard_map/ppermute | solution.py:34
  57.5 8.5 %collective-permute-done.9 = bf16[96,1536]{1,0:T(8,128)(2,1)S(1)} collective-permute-done((bf16[96,1536]{1,0:T(8,128)(2,1)S(1)}, bf16[96,1536]{1,0:T(8,128)(2,1)S(1)}, u32[]{:S(2)}, u32[]{:S(2)}) %collective-permute-start.9) | collective-permute-done | bytes 294944 | tf_op jit(solution)/shard_map/ppermute | solution.py:34
  65.9 2.1 %collective-permute-start.10 = (bf16[96,1536]{1,0:T(8,128)(2,1)S(1)}, bf16[96,1536]{1,0:T(8,128)(2,1)S(1)}, u32[]{:S(2)}, u32[]{:S(2)}) collective-permute-start(bf16[96,1536]{1,0:T(8,128)(2,1)S(1)} %constant_dynamic-slice_fusion), channel_id=1, source_target_pairs={{0,96},{32,128},{64,160},{96,192},{128,224},{160,0},{192,32},{224,... | collective-permute-start | bytes 884744 | tf_op jit(solution)/shard_map/ppermute | solution.py:34
  68.1 6.7 %collective-permute-done.10 = bf16[96,1536]{1,0:T(8,128)(2,1)S(1)} collective-permute-done((bf16[96,1536]{1,0:T(8,128)(2,1)S(1)}, bf16[96,1536]{1,0:T(8,128)(2,1)S(1)}, u32[]{:S(2)}, u32[]{:S(2)}) %collective-permute-start.10) | collective-permute-done | bytes 294944 | tf_op jit(solution)/shard_map/ppermute | solution.py:34
  74.9 3.1 %collective-permute-start.15 = (bf16[8,96,1536]{2,1,0:T(8,128)(2,1)S(1)}, bf16[8,96,1536]{2,1,0:T(8,128)(2,1)}, u32[]{:S(2)}, u32[]{:S(2)}) collective-permute-start(bf16[8,96,1536]{2,1,0:T(8,128)(2,1)S(1)} %bitcast_dynamic-update-slice_fusion.near), channel_id=1, source_target_pairs={{0,1},{1,0},{2,3},{3,2},{4,5},{5,4},{6,7},{7,6},{8,9},{9,8},{10,11... | collective-permute-start | bytes 7077896 | tf_op jit(solution)/shard_map/ppermute | solution.py:34
  78.0 2.8 %collective-permute-start.7 = (bf16[8,72,256]{2,1,0:T(8,128)(2,1)S(1)}, bf16[8,72,256]{2,1,0:T(8,128)(2,1)S(1)}, u32[]{:S(2)}, u32[]{:S(2)}) collective-permute-start(bf16[8,72,256]{2,1,0:T(8,128)(2,1)S(1)} %copy-done.7), channel_id=1, source_target_pairs={{0,2},{2,0},{1,3},{3,1},{4,6},{6,4},{5,7},{7,5},{8,10},{10,8},{9,1... | collective-permute-start | bytes 884744 | tf_op jit(solution)/shard_map/ppermute | solution.py:34
  80.8 7.3 %collective-permute-done.7.qb = bf16[8,72,256]{2,1,0:T(8,128)(2,1)S(1)} collective-permute-done((bf16[8,72,256]{2,1,0:T(8,128)(2,1)S(1)}, bf16[8,72,256]{2,1,0:T(8,128)(2,1)S(1)}, u32[]{:S(2)}, u32[]{:S(2)}) %collective-permute-start.7) | collective-permute-done | bytes 294944 | tf_op jit(solution)/shard_map/ppermute | solution.py:34
  88.8 2.6 %all-gather.3.cloned.1.call-done = bf16[128,72,384]{2,1,0:T(8,128)(2,1)} async-done(((bf16[8,72,384]{2,1,0:T(8,128)(2,1)}), bf16[128,72,384]{2,1,0:T(8,128)(2,1)}) %all-gather.3.cloned.1.call-update) | async-done | bytes 7077904 | tf_op jit(solution)/shard_map/all_gather | solution.py:423
  93.3 3.0 %attend_first.1 = bf16[8,2,72,256]{3,2,1,0:T(8,128)(2,1)S(1)} custom-call(s32[3]{0:T(128)S(1)} %pad_add_fusion.place, bf16[8,72,256]{2,1,0:T(8,128)(2,1)S(1)} %copy-done.8, bf16[8,72,256]{2,1,0:T(8,128)(2,1)S(1)} %copy-done.11, bf16[16,8,72,384]{3,2,1,0:T(8,128)(2,1)} %bitcast.45), custom_call_target="tpu_custom_call" | custom-call | flops 600000000 | bytes 2000000 | tf_op jit(solution)/shard_map/attend_first/pallas_call | solution.py:179
  97.1 6.6 %all-to-all-start.1 = ((bf16[16,72,256]{2,1,0:T(8,128)(2,1)}), bf16[16,72,256]{2,1,0:T(8,128)(2,1)}, u32[]{:S(2)}, u32[]{:S(2)}) async-start(bf16[16,72,256]{2,1,0:T(8,128)(2,1)} %bitcast.37), calls=%async_computation.1 | async-start | bytes 1179648 | tf_op jit(solution)/shard_map/all_to_all | solution.py:432
  105.7 29.6 %attend.1 = bf16[8,2,72,256]{3,2,1,0:T(8,128)(2,1)S(1)} custom-call(s32[3]{0:T(128)S(1)} %pad_add_fusion.place, s32[8,8]{1,0:T(8,128)S(1)} %copy-done.18, bf16[8,72,256]{2,1,0:T(8,128)(2,1)S(1)} %copy-done.9, bf16[8,72,256]{2,1,0:T(8,128)(2,1)S(1)} %copy-done.12, bf16[16,8,72,384]{3,2,1,0:T(8,128)(2,1)} %bitcast.46), custom_call_target="tpu_custom_call" | custom-call | flops 8000000000 | bytes 8000000 | tf_op jit(solution)/shard_map/attend/pallas_call | solution.py:298
  136.1 6.7 %all-to-all-start = ((bf16[16,72,256]{2,1,0:T(8,128)(2,1)}), bf16[16,72,256]{2,1,0:T(8,128)(2,1)}, u32[]{:S(2)}, u32[]{:S(2)}) async-start(bf16[16,72,256]{2,1,0:T(8,128)(2,1)} %bitcast.43), calls=%async_computation | async-start | bytes 1179648 | tf_op jit(solution)/shard_map/all_to_all | solution.py:436
  142.8 1.0 reshape.47.refs_0_
  143.8 1.0 copy-done.2
  145.7 4.5 %finish_first.1 = bf16[72,64]{1,0:T(8,128)(2,1)S(1)} custom-call(s32[3]{0:T(128)S(1)} %pad_add_fusion.place, s32[8]{0:T(128)S(1)} %copy-done.15, bf16[16,72,256]{2,1,0:T(8,128)(2,1)} %all-to-all-done.1.parts, bf16[8,96,1536]{2,1,0:T(8,128)(2,1)S(1)} %bitcast_dynamic-update-slice_fusion.near, bf16[8,96,1536]{2,1,0:T(8,128)(2,1)} %collective-permute-done.15.far, ...), custom_call_target="tpu_custom_call" | custom-call | flops 339738624 | bytes 6000000 | tf_op jit(solution)/shard_map/finish_first/pallas_call | solution.py:381
  150.7 6.0 %collective-permute-start.16 = (bf16[5,1,48,16]{2,3,1,0:T(8,128)(2,1)S(1)}, bf16[5,1,48,16]{2,3,1,0:T(8,128)(2,1)S(1)}, u32[]{:S(2)}, u32[]{:S(2)}) collective-permute-start(bf16[5,1,48,16]{2,3,1,0:T(8,128)(2,1)S(1)} %get-tuple-element.14), channel_id=1, source_target_pairs={{0,1},{1,2},{2,3},{3,4},{4,5},{5,6},{6,7},{7,8},{8,9},{9,10},{10,1... | collective-permute-start | bytes 23048 | tf_op jit(solution)/shard_map/ppermute | solution.py:456
  156.7 1.9 %collective-permute-start.17 = (bf16[5,1,48,16]{2,3,1,0:T(8,128)(2,1)S(1)}, bf16[5,1,48,16]{2,3,1,0:T(8,128)(2,1)S(1)}, u32[]{:S(2)}, u32[]{:S(2)}) collective-permute-start(bf16[5,1,48,16]{2,3,1,0:T(8,128)(2,1)S(1)} %get-tuple-element.15), channel_id=1, source_target_pairs={{1,0},{2,1},{3,2},{4,3},{5,4},{6,5},{7,6},{8,7},{9,8},{10,9},{11,1... | collective-permute-start | bytes 23048 | tf_op jit(solution)/shard_map/ppermute | solution.py:457
  159.6 4.8 %finish.1 = bf16[72,1536]{1,0:T(8,128)(2,1)} custom-call(s32[3]{0:T(128)S(1)} %pad_add_fusion.place, s32[8]{0:T(128)S(1)} %copy-done.15, bf16[16,72,256]{2,1,0:T(8,128)(2,1)} %all-to-all-done.parts, bf16[8,96,1536]{2,1,0:T(8,128)(2,1)S(1)} %bitcast_dynamic-update-slice_fusion.near, bf16[8,96,1536]{2,1,0:T(8,128)(2,1)} %collective-permute-done.15.far, ...), custom_call_target="tpu_custom_call" | custom-call | flops 339738624 | bytes 6000000 | tf_op jit(solution)/shard_map/finish/pallas_call | solution.py:381
  164.6 1.9 %fusion.1 = f32[1,3,2,6,384]{4,0,3,2,1:T(1,128)S(1)} fusion(bf16[3,3,3,16,384]{4,3,2,1,0:T(8,128)(2,1)} %bitcast.50, bf16[1,5,4,8,16]{4,3,2,1,0:T(8,128)(2,1)S(1)} %fusion.4), kind=kOutput, calls=%fused_computation.12 | convolution fusion | flops 11943936 | bytes 392192 | tf_op jit(solution)/shard_map/conv_general_dilated | solution.py:461
  (85 shorter events, 11.3 us)
Async XLA Ops:
  7.2 28.8 %copy-start = (bf16[192,1536]{1,0:T(8,128)(2,1)S(1)}, bf16[192,1536]{1,0:T(8,128)(2,1)}, u32[]{:S(2)}) copy-start(bf16[192,1536]{1,0:T(8,128)(2,1)} %param.16) | copy-start | bytes 1769476
  7.2 84.2 %all-gather.3.cloned.1.call-start = ((), (), s32[]{:S(2)}) async-start(), calls=%async_computation.2 | async-start | bytes 7520256 | tf_op jit(solution)/shard_map/all_gather | solution.py:423
  7.2 18.1 %collective-permute-start.2 = (bf16[72,1536]{1,0:T(8,128)(2,1)}, bf16[72,1536]{1,0:T(8,128)(2,1)S(1)}, u32[]{:S(2)}, u32[]{:S(2)}) collective-permute-start(bf16[72,1536]{1,0:T(8,128)(2,1)} %bitcast.38), channel_id=1, source_target_pairs={{0,192},{64,0},{128,64},{192,128},{1,193},{65,1},{129,65},{193,129... | collective-permute-start | bytes 663560 | tf_op jit(solution)/shard_map/ppermute | solution.py:34
  10.6 8.8 %collective-permute-start.1 = (bf16[72,1536]{1,0:T(8,128)(2,1)}, bf16[72,1536]{1,0:T(8,128)(2,1)S(1)}, u32[]{:S(2)}, u32[]{:S(2)}) collective-permute-start(bf16[72,1536]{1,0:T(8,128)(2,1)} %bitcast.39), channel_id=1, source_target_pairs={{0,64},{64,128},{128,192},{192,0},{1,65},{65,129},{129,193},{193,1... | collective-permute-start | bytes 663560 | tf_op jit(solution)/shard_map/ppermute | solution.py:34
  10.6 6.0 %collective-permute-start = (bf16[72,1536]{1,0:T(8,128)(2,1)}, bf16[72,1536]{1,0:T(8,128)(2,1)S(1)}, u32[]{:S(2)}, u32[]{:S(2)}) collective-permute-start(bf16[72,1536]{1,0:T(8,128)(2,1)} %bitcast.40), channel_id=1, source_target_pairs={{0,32},{32,0},{1,33},{33,1},{2,34},{34,2},{3,35},{35,3},{4,36},{36... | collective-permute-start | bytes 663560 | tf_op jit(solution)/shard_map/ppermute | solution.py:34
  13.0 1.5 copy-start.17
  14.5 15.5 %copy-start.3 = (bf16[1,72,1536]{2,1,0:T(8,128)(2,1)S(1)}, bf16[1,72,1536]{2,1,0:T(8,128)(2,1)}, u32[]{:S(2)}) copy-start(bf16[1,72,1536]{2,1,0:T(8,128)(2,1)} %param.11) | copy-start | bytes 663556
  14.5 15.5 %copy-start.15 = (s32[8]{0:T(128)S(1)}, s32[8]{0:T(128)}, u32[]{:S(2)}) copy-start(s32[8]{0:T(128)} %levels.5) | copy-start | bytes 100
  16.6 5.6 %collective-permute-start.4 = (bf16[72,1536]{1,0:T(8,128)(2,1)S(1)}, bf16[72,1536]{1,0:T(8,128)(2,1)S(1)}, u32[]{:S(2)}, u32[]{:S(2)}) collective-permute-start(bf16[72,1536]{1,0:T(8,128)(2,1)S(1)} %collective-permute-done.refs_1_), channel_id=1, source_target_pairs={{0,192},{64,0},{128,64},{192,128},{1,193},{65,1},{129,65},{193,129... | collective-permute-start | bytes 663560 | tf_op jit(solution)/shard_map/ppermute | solution.py:34
  19.4 10.6 %collective-permute-start.3 = (bf16[72,1536]{1,0:T(8,128)(2,1)S(1)}, bf16[72,1536]{1,0:T(8,128)(2,1)S(1)}, u32[]{:S(2)}, u32[]{:S(2)}) collective-permute-start(bf16[72,1536]{1,0:T(8,128)(2,1)S(1)} %collective-permute-done.refs_1_), channel_id=1, source_target_pairs={{0,64},{64,128},{128,192},{192,0},{1,65},{65,129},{129,193},{193,1... | collective-permute-start | bytes 663560 | tf_op jit(solution)/shard_map/ppermute | solution.py:34
  19.5 10.6 %collective-permute-start.5 = (bf16[72,1536]{1,0:T(8,128)(2,1)S(1)}, bf16[72,1536]{1,0:T(8,128)(2,1)S(1)}, u32[]{:S(2)}, u32[]{:S(2)}) collective-permute-start(bf16[72,1536]{1,0:T(8,128)(2,1)S(1)} %collective-permute-done.1.refs_2_), channel_id=1, source_target_pairs={{0,64},{64,128},{128,192},{192,0},{1,65},{65,129},{129,193},{193,1... | collective-permute-start | bytes 663560 | tf_op jit(solution)/shard_map/ppermute | solution.py:34
  22.2 7.8 %collective-permute-start.6 = (bf16[72,1536]{1,0:T(8,128)(2,1)S(1)}, bf16[72,1536]{1,0:T(8,128)(2,1)S(1)}, u32[]{:S(2)}, u32[]{:S(2)}) collective-permute-start(bf16[72,1536]{1,0:T(8,128)(2,1)S(1)} %collective-permute-done.4.refs_5_), channel_id=1, source_target_pairs={{0,192},{64,0},{128,64},{192,128},{1,193},{65,1},{129,65},{193,129... | collective-permute-start | bytes 663560 | tf_op jit(solution)/shard_map/ppermute | solution.py:34
  36.0 42.0 %copy-start.7 = (bf16[8,72,256]{2,1,0:T(8,128)(2,1)S(1)}, bf16[8,72,256]{2,1,0:T(8,128)(2,1)}, u32[]{:S(2)}) copy-start(bf16[8,72,256]{2,1,0:T(8,128)(2,1)} %copy-done.6) | copy-start | bytes 884740
  36.0 38.9 %collective-permute-start.14 = (bf16[96,1536]{1,0:T(8,128)(2,1)S(1)}, bf16[96,1536]{1,0:T(8,128)(2,1)S(1)}, u32[]{:S(2)}, u32[]{:S(2)}) collective-permute-start(bf16[96,1536]{1,0:T(8,128)(2,1)S(1)} %constant_dynamic-slice_fusion), channel_id=1, source_target_pairs={{0,224},{32,0},{64,32},{96,64},{128,96},{160,128},{192,160},{224,1... | collective-permute-start | bytes 884744 | tf_op jit(solution)/shard_map/ppermute | solution.py:34
  38.2 36.6 %collective-permute-start.13 = (bf16[96,1536]{1,0:T(8,128)(2,1)S(1)}, bf16[96,1536]{1,0:T(8,128)(2,1)S(1)}, u32[]{:S(2)}, u32[]{:S(2)}) collective-permute-start(bf16[96,1536]{1,0:T(8,128)(2,1)S(1)} %constant_dynamic-slice_fusion), channel_id=1, source_target_pairs={{0,192},{32,224},{64,0},{96,32},{128,64},{160,96},{192,128},{224,1... | collective-permute-start | bytes 884744 | tf_op jit(solution)/shard_map/ppermute | solution.py:34
  38.2 36.6 %collective-permute-start.12 = (bf16[96,1536]{1,0:T(8,128)(2,1)S(1)}, bf16[96,1536]{1,0:T(8,128)(2,1)S(1)}, u32[]{:S(2)}, u32[]{:S(2)}) collective-permute-start(bf16[96,1536]{1,0:T(8,128)(2,1)S(1)} %constant_dynamic-slice_fusion), channel_id=1, source_target_pairs={{0,160},{32,192},{64,224},{96,0},{128,32},{160,64},{192,96},{224,1... | collective-permute-start | bytes 884744 | tf_op jit(solution)/shard_map/ppermute | solution.py:34
  38.2 36.5 %collective-permute-start.11 = (bf16[96,1536]{1,0:T(8,128)(2,1)S(1)}, bf16[96,1536]{1,0:T(8,128)(2,1)S(1)}, u32[]{:S(2)}, u32[]{:S(2)}) collective-permute-start(bf16[96,1536]{1,0:T(8,128)(2,1)S(1)} %constant_dynamic-slice_fusion), channel_id=1, source_target_pairs={{0,128},{32,160},{64,192},{96,224},{128,0},{160,32},{192,64},{224,... | collective-permute-start | bytes 884744 | tf_op jit(solution)/shard_map/ppermute | solution.py:34
  41.5 15.9 %collective-permute-start.8 = (bf16[96,1536]{1,0:T(8,128)(2,1)S(1)}, bf16[96,1536]{1,0:T(8,128)(2,1)S(1)}, u32[]{:S(2)}, u32[]{:S(2)}) collective-permute-start(bf16[96,1536]{1,0:T(8,128)(2,1)S(1)} %constant_dynamic-slice_fusion), channel_id=1, source_target_pairs={{0,32},{32,64},{64,96},{96,128},{128,160},{160,192},{192,224},{224... | collective-permute-start | bytes 884744 | tf_op jit(solution)/shard_map/ppermute | solution.py:34
  57.4 8.5 %collective-permute-start.9 = (bf16[96,1536]{1,0:T(8,128)(2,1)S(1)}, bf16[96,1536]{1,0:T(8,128)(2,1)S(1)}, u32[]{:S(2)}, u32[]{:S(2)}) collective-permute-start(bf16[96,1536]{1,0:T(8,128)(2,1)S(1)} %constant_dynamic-slice_fusion), channel_id=1, source_target_pairs={{0,64},{32,96},{64,128},{96,160},{128,192},{160,224},{192,0},{224,... | collective-permute-start | bytes 884744 | tf_op jit(solution)/shard_map/ppermute | solution.py:34
  65.9 8.8 %collective-permute-start.10 = (bf16[96,1536]{1,0:T(8,128)(2,1)S(1)}, bf16[96,1536]{1,0:T(8,128)(2,1)S(1)}, u32[]{:S(2)}, u32[]{:S(2)}) collective-permute-start(bf16[96,1536]{1,0:T(8,128)(2,1)S(1)} %constant_dynamic-slice_fusion), channel_id=1, source_target_pairs={{0,96},{32,128},{64,160},{96,192},{128,224},{160,0},{192,32},{224,... | collective-permute-start | bytes 884744 | tf_op jit(solution)/shard_map/ppermute | solution.py:34
  74.9 68.8 %collective-permute-start.15 = (bf16[8,96,1536]{2,1,0:T(8,128)(2,1)S(1)}, bf16[8,96,1536]{2,1,0:T(8,128)(2,1)}, u32[]{:S(2)}, u32[]{:S(2)}) collective-permute-start(bf16[8,96,1536]{2,1,0:T(8,128)(2,1)S(1)} %bitcast_dynamic-update-slice_fusion.near), channel_id=1, source_target_pairs={{0,1},{1,0},{2,3},{3,2},{4,5},{5,4},{6,7},{7,6},{8,9},{9,8},{10,11... | collective-permute-start | bytes 7077896 | tf_op jit(solution)/shard_map/ppermute | solution.py:34
  78.0 10.1 %collective-permute-start.7 = (bf16[8,72,256]{2,1,0:T(8,128)(2,1)S(1)}, bf16[8,72,256]{2,1,0:T(8,128)(2,1)S(1)}, u32[]{:S(2)}, u32[]{:S(2)}) collective-permute-start(bf16[8,72,256]{2,1,0:T(8,128)(2,1)S(1)} %copy-done.7), channel_id=1, source_target_pairs={{0,2},{2,0},{1,3},{3,1},{4,6},{6,4},{5,7},{7,5},{8,10},{10,8},{9,1... | collective-permute-start | bytes 884744 | tf_op jit(solution)/shard_map/ppermute | solution.py:34
  93.3 10.4 %copy-start.18 = (s32[8,8]{1,0:T(8,128)S(1)}, s32[8,8]{1,0:T(8,128)}, u32[]{:S(2)}) copy-start(s32[8,8]{1,0:T(8,128)} %mask.1) | copy-start | bytes 772
  97.1 39.0 %all-to-all-start.1 = ((bf16[16,72,256]{2,1,0:T(8,128)(2,1)}), bf16[16,72,256]{2,1,0:T(8,128)(2,1)}, u32[]{:S(2)}, u32[]{:S(2)}) async-start(bf16[16,72,256]{2,1,0:T(8,128)(2,1)} %bitcast.37), calls=%async_computation.1 | async-start | bytes 1179648 | tf_op jit(solution)/shard_map/all_to_all | solution.py:432
  105.7 37.1 %copy-start.19 = (bf16[768,128]{1,0:T(8,128)(2,1)S(1)}, bf16[768,128]{1,0:T(8,128)(2,1)}, u32[]{:S(2)}) copy-start(bf16[768,128]{1,0:T(8,128)(2,1)} %param.17) | copy-start | bytes 589828
  105.7 38.1 %copy-start.16 = (f32[64]{0:T(128)S(1)}, f32[64]{0:T(128)}, u32[]{:S(2)}) copy-start(f32[64]{0:T(128)} %param.18) | copy-start | bytes 772
  136.1 22.5 %all-to-all-start = ((bf16[16,72,256]{2,1,0:T(8,128)(2,1)}), bf16[16,72,256]{2,1,0:T(8,128)(2,1)}, u32[]{:S(2)}, u32[]{:S(2)}) async-start(bf16[16,72,256]{2,1,0:T(8,128)(2,1)} %bitcast.43), calls=%async_computation | async-start | bytes 1179648 | tf_op jit(solution)/shard_map/all_to_all | solution.py:436
  143.8 1.0 copy-start.2
  145.7 5.0 %copy-start.20 = (bf16[2,2,48,16]{2,3,1,0:T(8,128)(2,1)S(1)}, bf16[2,2,48,16]{2,3,1,0:T(8,128)(2,1)}, u32[]{:S(2)}) copy-start(bf16[2,2,48,16]{2,3,1,0:T(8,128)(2,1)} %param.19) | copy-start | bytes 18436
  150.7 13.7 %collective-permute-start.16 = (bf16[5,1,48,16]{2,3,1,0:T(8,128)(2,1)S(1)}, bf16[5,1,48,16]{2,3,1,0:T(8,128)(2,1)S(1)}, u32[]{:S(2)}, u32[]{:S(2)}) collective-permute-start(bf16[5,1,48,16]{2,3,1,0:T(8,128)(2,1)S(1)} %get-tuple-element.14), channel_id=1, source_target_pairs={{0,1},{1,2},{2,3},{3,4},{4,5},{5,6},{6,7},{7,8},{8,9},{9,10},{10,1... | collective-permute-start | bytes 23048 | tf_op jit(solution)/shard_map/ppermute | solution.py:456
  156.7 7.7 %collective-permute-start.17 = (bf16[5,1,48,16]{2,3,1,0:T(8,128)(2,1)S(1)}, bf16[5,1,48,16]{2,3,1,0:T(8,128)(2,1)S(1)}, u32[]{:S(2)}, u32[]{:S(2)}) collective-permute-start(bf16[5,1,48,16]{2,3,1,0:T(8,128)(2,1)S(1)} %get-tuple-element.15), channel_id=1, source_target_pairs={{1,0},{2,1},{3,2},{4,3},{5,4},{6,5},{7,6},{8,7},{9,8},{10,9},{11,1... | collective-permute-start | bytes 23048 | tf_op jit(solution)/shard_map/ppermute | solution.py:457
  159.6 7.0 %copy-start.21 = (f32[384]{0:T(512)S(1)}, f32[384]{0:T(512)}, u32[]{:S(2)}) copy-start(f32[384]{0:T(512)} %param.21) | copy-start | bytes 4612
  (11 other events, 9.5 us)
Sparse Core Ops, SparseCore 0:
  36.1 55.2 all-gather.2

commit v3 on v2

--- a/solution.py
+++ b/solution.py
@@ -446,8 +446,6 @@
         head_weight.reshape(D, 4 * LCH),
         head_bias[None, :],
     )
-    hidden = finish(place, noise_steps, parts, near, far, own, modulation)
-
     latent = patches.reshape(LF, TCOL, 2, 2, LCH)
     latent = jnp.transpose(latent, (0, 2, 1, 3, 4)).reshape(LF, 2, 2 * TCOL, LCH)
     frames = jnp.concatenate([frame_cache, latent], axis=0)
@@ -467,6 +465,8 @@
         preferred_element_type=f32,
     )
     decoded = (product[0] + conv_bias).astype(bf16)
+    parts, decoded = lax.optimization_barrier((parts, decoded))
+    hidden = finish(place, noise_steps, parts, near, far, own, modulation)
     return (hidden[None], decoded)
 
 

time: 174 us -> 175 us (level); the launches traced: 174 us -> 173 us
  local copies, waits for them, and re-layouts: 14.8 us -> 11 us
  starting transfers between devices: 46.5 us -> 49.2 us
    ppermute x16, waiting for transfers between devices: 44.5 us -> 32 us  [shift(): lax.ppermute(block, axis, [(i, (i + step) % count) for i in range(count)])]
    all_gather x1, waiting for transfers between devices: 2.57 us -> 10.7 us  [per_device(): kv = lax.all_gather(kv_own, ('z', 'core'))]
    all_to_all x1, waiting for transfers between devices: 0.01 us -> 5.95 us  [per_device(): lax.all_to_all(partial.reshape(2 * SPANS, ROWS, LANES), SPAN + ('yhi',),...]
    unnamed x52 -> x38, local copies, waits for them, and re-layouts: 13.2 us -> 7.92 us
    ppermute x16, starting transfers between devices: 25.3 us -> 27.9 us  [shift(): lax.ppermute(block, axis, [(i, (i + step) % count) for i in range(count)])]
  transfers between devices with their start and end apart: 21 -> 21, of which waited for: 7 -> 9; matrix products, arithmetic and copies ran while one was open for 2% -> 4% of each run, Pallas kernels for 25% -> 19%
where the time goes in v3:
time: 175 us; the launch traced here: 173 us
  starting transfers between devices  49.2 us (28%)
  waiting for transfers between devices  48.7 us (28%)
  Pallas kernels  47.2 us (27%)
  between operations  14.4 us (8%)
  local copies, waits for them, and re-layouts  11 us (6%)
  matrix products  1.92 us (1%)
    ppermute x16, waiting for transfers between devices, shift(): lax.ppermute(block, axis, [(i, (i + step) % count) for i in range(count)])  32 us
    pallas_call x1, Pallas kernels, attend(): pl.pallas_call(attend_kernel, grid=(SPANS,), out_shape=jax.ShapeDtypeStru...  28.2 us
    ppermute x16, starting transfers between devices, shift(): lax.ppermute(block, axis, [(i, (i + step) % count) for i in range(count)])  27.9 us
    all_gather x1, waiting for transfers between devices, per_device(): kv = lax.all_gather(kv_own, ('z', 'core'))  10.7 us
    pallas_call x2, Pallas kernels, finish(): pl.pallas_call(functools.partial(finish_kernel, decode=decode), out_shape...  9.34 us
    unnamed x38, local copies, waits for them, and re-layouts  7.92 us
    all_to_all x1, starting transfers between devices, per_device(): lax.all_to_all(partial.reshape(2 * SPANS, ROWS, LANES), SPAN + ('yhi',),...  7.27 us
    all_to_all x1, starting transfers between devices, per_device(): lax.all_to_all(first_partial.reshape(2 * SPANS, ROWS, LANES), SPAN + ('yh...  6.58 us
  transfers between devices with their start and end apart: 21, of which 9 were waited for; matrix products, arithmetic and copies ran while one was open for 4% of the time, Pallas kernels for 19%

profile of v3, /device:TPU:1, one launch (start us, length us, event | category | flops | bytes accessed | tf_op | source)
XLA Modules:
  0.0 173.2 jit_solution(6979112853682467865)
XLA Ops:
  7.2 2.2 %collective-permute-start = (bf16[72,1536]{1,0:T(8,128)(2,1)}, bf16[72,1536]{1,0:T(8,128)(2,1)S(1)}, u32[]{:S(2)}, u32[]{:S(2)}) collective-permute-start(bf16[72,1536]{1,0:T(8,128)(2,1)} %bitcast.38), channel_id=1, source_target_pairs={{0,32},{32,0},{1,33},{33,1},{2,34},{34,2},{3,35},{35,3},{4,36},{36... | collective-permute-start | bytes 663560 | tf_op jit(solution)/shard_map/ppermute | solution.py:34
  9.4 1.2 collective-permute-start.1
  10.6 1.5 collective-permute-start.2
  12.1 1.1 copy.26.mod
  13.2 1.5 copy-done.10
  14.7 2.1 %arrange.1.weight = bf16[1536,640]{1,0:T(8,128)(2,1)S(1)} custom-call(bf16[768,1152]{1,0:T(8,128)(2,1)S(1)} %copy-done.10), custom_call_target="tpu_custom_call" | custom-call | flops 4000000000 | bytes 4000000 | tf_op jit(solution)/shard_map/arrange/pallas_call | solution.py:96
  16.8 1.3 collective-permute-start.4
  18.5 3.5 %collective-permute-done.4.refs_5_ = bf16[72,1536]{1,0:T(8,128)(2,1)S(1)} collective-permute-done((bf16[72,1536]{1,0:T(8,128)(2,1)S(1)}, bf16[72,1536]{1,0:T(8,128)(2,1)S(1)}, u32[]{:S(2)}, u32[]{:S(2)}) %collective-permute-start.4) | collective-permute-done | bytes 221216 | tf_op jit(solution)/shard_map/ppermute | solution.py:34
  22.0 2.7 %collective-permute-start.6 = (bf16[72,1536]{1,0:T(8,128)(2,1)S(1)}, bf16[72,1536]{1,0:T(8,128)(2,1)S(1)}, u32[]{:S(2)}, u32[]{:S(2)}) collective-permute-start(bf16[72,1536]{1,0:T(8,128)(2,1)S(1)} %collective-permute-done.4.refs_5_), channel_id=1, source_target_pairs={{0,192},{64,0},{128,64},{192,128},{1,193},{65,1},{129,65},{193,129... | collective-permute-start | bytes 663560 | tf_op jit(solution)/shard_map/ppermute | solution.py:34
  24.8 4.5 %collective-permute-done.5.refs_6_ = bf16[72,1536]{1,0:T(8,128)(2,1)S(1)} collective-permute-done((bf16[72,1536]{1,0:T(8,128)(2,1)S(1)}, bf16[72,1536]{1,0:T(8,128)(2,1)S(1)}, u32[]{:S(2)}, u32[]{:S(2)}) %collective-permute-start.5) | collective-permute-done | bytes 221216 | tf_op jit(solution)/shard_map/ppermute | solution.py:34
  29.3 4.6 %qkv.1 = (bf16[8,72,256]{2,1,0:T(8,128)(2,1)}, bf16[8,72,384]{2,1,0:T(8,128)(2,1)}, bf16[72,1536]{1,0:T(8,128)(2,1)S(1)}) custom-call(s32[3]{0:T(128)S(1)} %pad_add_fusion.place, s32[8]{0:T(128)S(1)} %copy-done.8, f32[8,5,1536]{2,1,0:T(8,128)S(1)} %copy.26.mod, bf16[256,256]{1,0:T(8,128)(2,1)S(1)} %fusion.perm, bf16[1536,640]{1,0:T(8,128)(2,1)S(1)} %arrange.1.weight, ...), custom_call_target="tpu_custom_call" | custom-call | flops 1132462080 | bytes 4500000 | tf_op jit(solution)/shard_map/qkv/pallas_call | solution.py:114
  35.0 2.9 %collective-permute-start.10 = (bf16[96,1536]{1,0:T(8,128)(2,1)S(1)}, bf16[96,1536]{1,0:T(8,128)(2,1)S(1)}, u32[]{:S(2)}, u32[]{:S(2)}) collective-permute-start(bf16[96,1536]{1,0:T(8,128)(2,1)S(1)} %constant_dynamic-slice_fusion), channel_id=1, source_target_pairs={{0,96},{32,128},{64,160},{96,192},{128,224},{160,0},{192,32},{224,... | collective-permute-start | bytes 884744 | tf_op jit(solution)/shard_map/ppermute | solution.py:34
  37.9 1.6 collective-permute-start.11
  39.5 2.0 %collective-permute-start.12 = (bf16[96,1536]{1,0:T(8,128)(2,1)S(1)}, bf16[96,1536]{1,0:T(8,128)(2,1)S(1)}, u32[]{:S(2)}, u32[]{:S(2)}) collective-permute-start(bf16[96,1536]{1,0:T(8,128)(2,1)S(1)} %constant_dynamic-slice_fusion), channel_id=1, source_target_pairs={{0,160},{32,192},{64,224},{96,0},{128,32},{160,64},{192,96},{224,1... | collective-permute-start | bytes 884744 | tf_op jit(solution)/shard_map/ppermute | solution.py:34
  42.8 5.7 %collective-permute-start.14 = (bf16[96,1536]{1,0:T(8,128)(2,1)S(1)}, bf16[96,1536]{1,0:T(8,128)(2,1)S(1)}, u32[]{:S(2)}, u32[]{:S(2)}) collective-permute-start(bf16[96,1536]{1,0:T(8,128)(2,1)S(1)} %constant_dynamic-slice_fusion), channel_id=1, source_target_pairs={{0,224},{32,0},{64,32},{96,64},{128,96},{160,128},{192,160},{224,1... | collective-permute-start | bytes 884744 | tf_op jit(solution)/shard_map/ppermute | solution.py:34
  48.6 6.2 %collective-permute-done.10 = bf16[96,1536]{1,0:T(8,128)(2,1)S(1)} collective-permute-done((bf16[96,1536]{1,0:T(8,128)(2,1)S(1)}, bf16[96,1536]{1,0:T(8,128)(2,1)S(1)}, u32[]{:S(2)}, u32[]{:S(2)}) %collective-permute-start.10) | collective-permute-done | bytes 294944 | tf_op jit(solution)/shard_map/ppermute | solution.py:34
  54.8 1.6 collective-permute-done.12
  56.5 8.8 %collective-permute-done.14 = bf16[96,1536]{1,0:T(8,128)(2,1)S(1)} collective-permute-done((bf16[96,1536]{1,0:T(8,128)(2,1)S(1)}, bf16[96,1536]{1,0:T(8,128)(2,1)S(1)}, u32[]{:S(2)}, u32[]{:S(2)}) %collective-permute-start.14) | collective-permute-done | bytes 294944 | tf_op jit(solution)/shard_map/ppermute | solution.py:34
  65.3 2.8 %collective-permute-start.15 = (bf16[8,96,1536]{2,1,0:T(8,128)(2,1)S(1)}, bf16[8,96,1536]{2,1,0:T(8,128)(2,1)}, u32[]{:S(2)}, u32[]{:S(2)}) collective-permute-start(bf16[8,96,1536]{2,1,0:T(8,128)(2,1)S(1)} %bitcast_dynamic-update-slice_fusion.near), channel_id=1, source_target_pairs={{0,1},{1,0},{2,3},{3,2},{4,5},{5,4},{6,7},{7,6},{8,9},{9,8},{10,11... | collective-permute-start | bytes 7077896 | tf_op jit(solution)/shard_map/ppermute | solution.py:34
  68.1 3.0 %collective-permute-start.7 = (bf16[8,72,256]{2,1,0:T(8,128)(2,1)}, bf16[8,72,256]{2,1,0:T(8,128)(2,1)}, u32[]{:S(2)}, u32[]{:S(2)}) collective-permute-start(bf16[8,72,256]{2,1,0:T(8,128)(2,1)} %get-tuple-element.9.qa), channel_id=1, source_target_pairs={{0,2},{2,0},{1,3},{3,1},{4,6},{6,4},{5,7},{7,5},{8,10},{10,8},{9,1... | collective-permute-start | bytes 884744 | tf_op jit(solution)/shard_map/ppermute | solution.py:34
  72.0 6.5 %collective-permute-done.7.qb = bf16[8,72,256]{2,1,0:T(8,128)(2,1)} collective-permute-done((bf16[8,72,256]{2,1,0:T(8,128)(2,1)}, bf16[8,72,256]{2,1,0:T(8,128)(2,1)}, u32[]{:S(2)}, u32[]{:S(2)}) %collective-permute-start.7) | collective-permute-done | bytes 294944 | tf_op jit(solution)/shard_map/ppermute | solution.py:34
  78.5 10.7 %all-gather.3.cloned.1.call-done = bf16[128,72,384]{2,1,0:T(8,128)(2,1)} async-done(((bf16[8,72,384]{2,1,0:T(8,128)(2,1)}), bf16[128,72,384]{2,1,0:T(8,128)(2,1)}) %all-gather.3.cloned.1.call-update) | async-done | bytes 7077904 | tf_op jit(solution)/shard_map/all_gather | solution.py:423
  89.2 3.0 %attend_first.1 = bf16[8,2,72,256]{3,2,1,0:T(8,128)(2,1)S(1)} custom-call(s32[3]{0:T(128)S(1)} %pad_add_fusion.place, bf16[8,72,256]{2,1,0:T(8,128)(2,1)} %get-tuple-element.9.qa, bf16[8,72,256]{2,1,0:T(8,128)(2,1)} %collective-permute-done.7.qb, bf16[16,8,72,384]{3,2,1,0:T(8,128)(2,1)} %bitcast.45), custom_call_target="tpu_custom_call" | custom-call | flops 600000000 | bytes 2000000 | tf_op jit(solution)/shard_map/attend_first/pallas_call | solution.py:179
  93.1 6.6 %all-to-all-start.1 = ((bf16[16,72,256]{2,1,0:T(8,128)(2,1)}), bf16[16,72,256]{2,1,0:T(8,128)(2,1)}, u32[]{:S(2)}, u32[]{:S(2)}) async-start(bf16[16,72,256]{2,1,0:T(8,128)(2,1)} %bitcast.37), calls=%async_computation.1 | async-start | bytes 1179648 | tf_op jit(solution)/shard_map/all_to_all | solution.py:432
  99.7 28.2 %attend.1 = bf16[8,2,72,256]{3,2,1,0:T(8,128)(2,1)S(1)} custom-call(s32[3]{0:T(128)S(1)} %pad_add_fusion.place, s32[8,8]{1,0:T(8,128)S(1)} %copy-done.11, bf16[8,72,256]{2,1,0:T(8,128)(2,1)} %get-tuple-element.9.qa, bf16[8,72,256]{2,1,0:T(8,128)(2,1)} %collective-permute-done.7.qb, bf16[16,8,72,384]{3,2,1,0:T(8,128)(2,1)} %bitcast.46), custom_call_target="tpu_custom_call" | custom-call | flops 8000000000 | bytes 8000000 | tf_op jit(solution)/shard_map/attend/pallas_call | solution.py:298
  130.6 4.5 %finish_first.1 = bf16[72,64]{1,0:T(8,128)(2,1)S(1)} custom-call(s32[3]{0:T(128)S(1)} %pad_add_fusion.place, s32[8]{0:T(128)S(1)} %copy-done.8, bf16[16,72,256]{2,1,0:T(8,128)(2,1)} %all-to-all-done.1.parts, bf16[8,96,1536]{2,1,0:T(8,128)(2,1)S(1)} %bitcast_dynamic-update-slice_fusion.near, bf16[8,96,1536]{2,1,0:T(8,128)(2,1)} %collective-permute-done.15.far, ...), custom_call_target="tpu_custom_call" | custom-call | flops 339738624 | bytes 6000000 | tf_op jit(solution)/shard_map/finish_first/pallas_call | solution.py:381
  135.6 2.4 %collective-permute-start.17 = (bf16[5,1,48,16]{2,3,1,0:T(8,128)(2,1)S(1)}, bf16[5,1,48,16]{2,3,1,0:T(8,128)(2,1)S(1)}, u32[]{:S(2)}, u32[]{:S(2)}) collective-permute-start(bf16[5,1,48,16]{2,3,1,0:T(8,128)(2,1)S(1)} %get-tuple-element.19), channel_id=1, source_target_pairs={{1,0},{2,1},{3,2},{4,3},{5,4},{6,5},{7,6},{8,7},{9,8},{10,9},{11,1... | collective-permute-start | bytes 23048 | tf_op jit(solution)/shard_map/ppermute | solution.py:455
  138.1 4.9 %collective-permute-start.16 = (bf16[5,1,48,16]{2,3,1,0:T(8,128)(2,1)S(1)}, bf16[5,1,48,16]{2,3,1,0:T(8,128)(2,1)S(1)}, u32[]{:S(2)}, u32[]{:S(2)}) collective-permute-start(bf16[5,1,48,16]{2,3,1,0:T(8,128)(2,1)S(1)} %get-tuple-element.18), channel_id=1, source_target_pairs={{0,1},{1,2},{2,3},{3,4},{4,5},{5,6},{6,7},{7,8},{8,9},{9,10},{10,1... | collective-permute-start | bytes 23048 | tf_op jit(solution)/shard_map/ppermute | solution.py:454
  143.0 7.3 %all-to-all-start = ((bf16[16,72,256]{2,1,0:T(8,128)(2,1)}), bf16[16,72,256]{2,1,0:T(8,128)(2,1)}, u32[]{:S(2)}, u32[]{:S(2)}) async-start(bf16[16,72,256]{2,1,0:T(8,128)(2,1)} %bitcast.43), calls=%async_computation | async-start | bytes 1179648 | tf_op jit(solution)/shard_map/all_to_all | solution.py:436
  152.1 1.9 %fusion.1 = f32[1,3,2,6,384]{4,0,3,2,1:T(1,128)S(1)} fusion(bf16[3,3,3,16,384]{4,3,2,1,0:T(8,128)(2,1)} %bitcast.50, bf16[1,5,4,8,16]{4,3,2,1,0:T(8,128)(2,1)S(1)} %fusion.4), kind=kOutput, calls=%fused_computation.12 | convolution fusion | flops 11943936 | bytes 392192 | tf_op jit(solution)/shard_map/conv_general_dilated | solution.py:459
  154.6 5.9 %all-to-all-done.parts = bf16[16,72,256]{2,1,0:T(8,128)(2,1)} async-done(((bf16[16,72,256]{2,1,0:T(8,128)(2,1)}), bf16[16,72,256]{2,1,0:T(8,128)(2,1)}, u32[]{:S(2)}, u32[]{:S(2)}) %all-to-all-start) | async-done | bytes 589856 | tf_op jit(solution)/shard_map/all_to_all | solution.py:436
  161.5 4.8 %finish.1 = bf16[72,1536]{1,0:T(8,128)(2,1)} custom-call(s32[3]{0:T(128)S(1)} %pad_add_fusion.place, s32[8]{0:T(128)S(1)} %copy-done.8, bf16[16,72,256]{2,1,0:T(8,128)(2,1)} %all-to-all-done.parts, bf16[8,96,1536]{2,1,0:T(8,128)(2,1)S(1)} %bitcast_dynamic-update-slice_fusion.near, bf16[8,96,1536]{2,1,0:T(8,128)(2,1)} %collective-permute-done.15.far, ...), custom_call_target="tpu_custom_call" | custom-call | flops 339738624 | bytes 6000000 | tf_op jit(solution)/shard_map/finish/pallas_call | solution.py:381
  (71 shorter events, 11.3 us)
Async XLA Ops:
  7.2 27.5 %copy-start = (bf16[192,1536]{1,0:T(8,128)(2,1)S(1)}, bf16[192,1536]{1,0:T(8,128)(2,1)}, u32[]{:S(2)}) copy-start(bf16[192,1536]{1,0:T(8,128)(2,1)} %param.16) | copy-start | bytes 1769476
  7.2 82.0 %all-gather.3.cloned.1.call-start = ((), (), s32[]{:S(2)}) async-start(), calls=%async_computation.2 | async-start | bytes 7520256 | tf_op jit(solution)/shard_map/all_gather | solution.py:423
  7.2 9.6 %collective-permute-start = (bf16[72,1536]{1,0:T(8,128)(2,1)}, bf16[72,1536]{1,0:T(8,128)(2,1)S(1)}, u32[]{:S(2)}, u32[]{:S(2)}) collective-permute-start(bf16[72,1536]{1,0:T(8,128)(2,1)} %bitcast.38), channel_id=1, source_target_pairs={{0,32},{32,0},{1,33},{33,1},{2,34},{34,2},{3,35},{35,3},{4,36},{36... | collective-permute-start | bytes 663560 | tf_op jit(solution)/shard_map/ppermute | solution.py:34
  9.4 9.0 %collective-permute-start.1 = (bf16[72,1536]{1,0:T(8,128)(2,1)}, bf16[72,1536]{1,0:T(8,128)(2,1)S(1)}, u32[]{:S(2)}, u32[]{:S(2)}) collective-permute-start(bf16[72,1536]{1,0:T(8,128)(2,1)} %bitcast.39), channel_id=1, source_target_pairs={{0,64},{64,128},{128,192},{192,0},{1,65},{65,129},{129,193},{193,1... | collective-permute-start | bytes 663560 | tf_op jit(solution)/shard_map/ppermute | solution.py:34
  10.6 14.1 %collective-permute-start.2 = (bf16[72,1536]{1,0:T(8,128)(2,1)}, bf16[72,1536]{1,0:T(8,128)(2,1)S(1)}, u32[]{:S(2)}, u32[]{:S(2)}) collective-permute-start(bf16[72,1536]{1,0:T(8,128)(2,1)} %bitcast.40), channel_id=1, source_target_pairs={{0,192},{64,0},{128,64},{192,128},{1,193},{65,1},{129,65},{193,129... | collective-permute-start | bytes 663560 | tf_op jit(solution)/shard_map/ppermute | solution.py:34
  13.2 1.5 copy-start.10
  14.7 14.6 %copy-start.3 = (bf16[1,72,1536]{2,1,0:T(8,128)(2,1)S(1)}, bf16[1,72,1536]{2,1,0:T(8,128)(2,1)}, u32[]{:S(2)}) copy-start(bf16[1,72,1536]{2,1,0:T(8,128)(2,1)} %param.11) | copy-start | bytes 663556
  14.7 14.6 %copy-start.8 = (s32[8]{0:T(128)S(1)}, s32[8]{0:T(128)}, u32[]{:S(2)}) copy-start(s32[8]{0:T(128)} %levels.5) | copy-start | bytes 100
  16.8 5.2 %collective-permute-start.4 = (bf16[72,1536]{1,0:T(8,128)(2,1)S(1)}, bf16[72,1536]{1,0:T(8,128)(2,1)S(1)}, u32[]{:S(2)}, u32[]{:S(2)}) collective-permute-start(bf16[72,1536]{1,0:T(8,128)(2,1)S(1)} %collective-permute-done.refs_1_), channel_id=1, source_target_pairs={{0,192},{64,0},{128,64},{192,128},{1,193},{65,1},{129,65},{193,129... | collective-permute-start | bytes 663560 | tf_op jit(solution)/shard_map/ppermute | solution.py:34
  18.2 6.6 %collective-permute-start.3 = (bf16[72,1536]{1,0:T(8,128)(2,1)S(1)}, bf16[72,1536]{1,0:T(8,128)(2,1)S(1)}, u32[]{:S(2)}, u32[]{:S(2)}) collective-permute-start(bf16[72,1536]{1,0:T(8,128)(2,1)S(1)} %collective-permute-done.refs_1_), channel_id=1, source_target_pairs={{0,64},{64,128},{128,192},{192,0},{1,65},{65,129},{129,193},{193,1... | collective-permute-start | bytes 663560 | tf_op jit(solution)/shard_map/ppermute | solution.py:34
  18.4 10.9 %collective-permute-start.5 = (bf16[72,1536]{1,0:T(8,128)(2,1)S(1)}, bf16[72,1536]{1,0:T(8,128)(2,1)S(1)}, u32[]{:S(2)}, u32[]{:S(2)}) collective-permute-start(bf16[72,1536]{1,0:T(8,128)(2,1)S(1)} %collective-permute-done.1.refs_2_), channel_id=1, source_target_pairs={{0,64},{64,128},{128,192},{192,0},{1,65},{65,129},{129,193},{193,1... | collective-permute-start | bytes 663560 | tf_op jit(solution)/shard_map/ppermute | solution.py:34
  22.0 7.3 %collective-permute-start.6 = (bf16[72,1536]{1,0:T(8,128)(2,1)S(1)}, bf16[72,1536]{1,0:T(8,128)(2,1)S(1)}, u32[]{:S(2)}, u32[]{:S(2)}) collective-permute-start(bf16[72,1536]{1,0:T(8,128)(2,1)S(1)} %collective-permute-done.4.refs_5_), channel_id=1, source_target_pairs={{0,192},{64,0},{128,64},{192,128},{1,193},{65,1},{129,65},{193,129... | collective-permute-start | bytes 663560 | tf_op jit(solution)/shard_map/ppermute | solution.py:34
  34.7 36.4 %copy-start.12 = (bf16[768,128]{1,0:T(8,128)(2,1)S(1)}, bf16[768,128]{1,0:T(8,128)(2,1)}, u32[]{:S(2)}) copy-start(bf16[768,128]{1,0:T(8,128)(2,1)} %param.17) | copy-start | bytes 589828
  34.7 7.8 %collective-permute-start.8 = (bf16[96,1536]{1,0:T(8,128)(2,1)S(1)}, bf16[96,1536]{1,0:T(8,128)(2,1)S(1)}, u32[]{:S(2)}, u32[]{:S(2)}) collective-permute-start(bf16[96,1536]{1,0:T(8,128)(2,1)S(1)} %constant_dynamic-slice_fusion), channel_id=1, source_target_pairs={{0,32},{32,64},{64,96},{96,128},{128,160},{160,192},{192,224},{224... | collective-permute-start | bytes 884744 | tf_op jit(solution)/shard_map/ppermute | solution.py:34
  35.0 7.9 %collective-permute-start.9 = (bf16[96,1536]{1,0:T(8,128)(2,1)S(1)}, bf16[96,1536]{1,0:T(8,128)(2,1)S(1)}, u32[]{:S(2)}, u32[]{:S(2)}) collective-permute-start(bf16[96,1536]{1,0:T(8,128)(2,1)S(1)} %constant_dynamic-slice_fusion), channel_id=1, source_target_pairs={{0,64},{32,96},{64,128},{96,160},{128,192},{160,224},{192,0},{224,... | collective-permute-start | bytes 884744 | tf_op jit(solution)/shard_map/ppermute | solution.py:34
  35.0 19.7 %collective-permute-start.10 = (bf16[96,1536]{1,0:T(8,128)(2,1)S(1)}, bf16[96,1536]{1,0:T(8,128)(2,1)S(1)}, u32[]{:S(2)}, u32[]{:S(2)}) collective-permute-start(bf16[96,1536]{1,0:T(8,128)(2,1)S(1)} %constant_dynamic-slice_fusion), channel_id=1, source_target_pairs={{0,96},{32,128},{64,160},{96,192},{128,224},{160,0},{192,32},{224,... | collective-permute-start | bytes 884744 | tf_op jit(solution)/shard_map/ppermute | solution.py:34
  37.9 16.8 %collective-permute-start.11 = (bf16[96,1536]{1,0:T(8,128)(2,1)S(1)}, bf16[96,1536]{1,0:T(8,128)(2,1)S(1)}, u32[]{:S(2)}, u32[]{:S(2)}) collective-permute-start(bf16[96,1536]{1,0:T(8,128)(2,1)S(1)} %constant_dynamic-slice_fusion), channel_id=1, source_target_pairs={{0,128},{32,160},{64,192},{96,224},{128,0},{160,32},{192,64},{224,... | collective-permute-start | bytes 884744 | tf_op jit(solution)/shard_map/ppermute | solution.py:34
  39.5 16.9 %collective-permute-start.12 = (bf16[96,1536]{1,0:T(8,128)(2,1)S(1)}, bf16[96,1536]{1,0:T(8,128)(2,1)S(1)}, u32[]{:S(2)}, u32[]{:S(2)}) collective-permute-start(bf16[96,1536]{1,0:T(8,128)(2,1)S(1)} %constant_dynamic-slice_fusion), channel_id=1, source_target_pairs={{0,160},{32,192},{64,224},{96,0},{128,32},{160,64},{192,96},{224,1... | collective-permute-start | bytes 884744 | tf_op jit(solution)/shard_map/ppermute | solution.py:34
  42.4 14.0 %collective-permute-start.13 = (bf16[96,1536]{1,0:T(8,128)(2,1)S(1)}, bf16[96,1536]{1,0:T(8,128)(2,1)S(1)}, u32[]{:S(2)}, u32[]{:S(2)}) collective-permute-start(bf16[96,1536]{1,0:T(8,128)(2,1)S(1)} %constant_dynamic-slice_fusion), channel_id=1, source_target_pairs={{0,192},{32,224},{64,0},{96,32},{128,64},{160,96},{192,128},{224,1... | collective-permute-start | bytes 884744 | tf_op jit(solution)/shard_map/ppermute | solution.py:34
  42.8 22.5 %collective-permute-start.14 = (bf16[96,1536]{1,0:T(8,128)(2,1)S(1)}, bf16[96,1536]{1,0:T(8,128)(2,1)S(1)}, u32[]{:S(2)}, u32[]{:S(2)}) collective-permute-start(bf16[96,1536]{1,0:T(8,128)(2,1)S(1)} %constant_dynamic-slice_fusion), channel_id=1, source_target_pairs={{0,224},{32,0},{64,32},{96,64},{128,96},{160,128},{192,160},{224,1... | collective-permute-start | bytes 884744 | tf_op jit(solution)/shard_map/ppermute | solution.py:34
  65.3 63.4 %collective-permute-start.15 = (bf16[8,96,1536]{2,1,0:T(8,128)(2,1)S(1)}, bf16[8,96,1536]{2,1,0:T(8,128)(2,1)}, u32[]{:S(2)}, u32[]{:S(2)}) collective-permute-start(bf16[8,96,1536]{2,1,0:T(8,128)(2,1)S(1)} %bitcast_dynamic-update-slice_fusion.near), channel_id=1, source_target_pairs={{0,1},{1,0},{2,3},{3,2},{4,5},{5,4},{6,7},{7,6},{8,9},{9,8},{10,11... | collective-permute-start | bytes 7077896 | tf_op jit(solution)/shard_map/ppermute | solution.py:34
  68.1 10.4 %collective-permute-start.7 = (bf16[8,72,256]{2,1,0:T(8,128)(2,1)}, bf16[8,72,256]{2,1,0:T(8,128)(2,1)}, u32[]{:S(2)}, u32[]{:S(2)}) collective-permute-start(bf16[8,72,256]{2,1,0:T(8,128)(2,1)} %get-tuple-element.9.qa), channel_id=1, source_target_pairs={{0,2},{2,0},{1,3},{3,1},{4,6},{6,4},{5,7},{7,5},{8,10},{10,8},{9,1... | collective-permute-start | bytes 884744 | tf_op jit(solution)/shard_map/ppermute | solution.py:34
  89.2 10.4 %copy-start.11 = (s32[8,8]{1,0:T(8,128)S(1)}, s32[8,8]{1,0:T(8,128)}, u32[]{:S(2)}) copy-start(s32[8,8]{1,0:T(8,128)} %mask.1) | copy-start | bytes 772
  93.1 35.6 %all-to-all-start.1 = ((bf16[16,72,256]{2,1,0:T(8,128)(2,1)}), bf16[16,72,256]{2,1,0:T(8,128)(2,1)}, u32[]{:S(2)}, u32[]{:S(2)}) async-start(bf16[16,72,256]{2,1,0:T(8,128)(2,1)} %bitcast.37), calls=%async_computation.1 | async-start | bytes 1179648 | tf_op jit(solution)/shard_map/all_to_all | solution.py:432
  99.7 29.0 %copy-start.9 = (f32[64]{0:T(128)S(1)}, f32[64]{0:T(128)}, u32[]{:S(2)}) copy-start(f32[64]{0:T(128)} %param.18) | copy-start | bytes 772
  128.7 1.0 copy-start.2
  130.6 5.0 %copy-start.13 = (bf16[2,2,48,16]{2,3,1,0:T(8,128)(2,1)S(1)}, bf16[2,2,48,16]{2,3,1,0:T(8,128)(2,1)}, u32[]{:S(2)}) copy-start(bf16[2,2,48,16]{2,3,1,0:T(8,128)(2,1)} %param.19) | copy-start | bytes 18436
  135.2 18.8 %copy-start.14 = (f32[384]{0:T(512)S(1)}, f32[384]{0:T(512)}, u32[]{:S(2)}) copy-start(f32[384]{0:T(512)} %param.21) | copy-start | bytes 4612
  135.6 14.6 %collective-permute-start.17 = (bf16[5,1,48,16]{2,3,1,0:T(8,128)(2,1)S(1)}, bf16[5,1,48,16]{2,3,1,0:T(8,128)(2,1)S(1)}, u32[]{:S(2)}, u32[]{:S(2)}) collective-permute-start(bf16[5,1,48,16]{2,3,1,0:T(8,128)(2,1)S(1)} %get-tuple-element.19), channel_id=1, source_target_pairs={{1,0},{2,1},{3,2},{4,3},{5,4},{6,5},{7,6},{8,7},{9,8},{10,9},{11,1... | collective-permute-start | bytes 23048 | tf_op jit(solution)/shard_map/ppermute | solution.py:455
  138.1 12.2 %collective-permute-start.16 = (bf16[5,1,48,16]{2,3,1,0:T(8,128)(2,1)S(1)}, bf16[5,1,48,16]{2,3,1,0:T(8,128)(2,1)S(1)}, u32[]{:S(2)}, u32[]{:S(2)}) collective-permute-start(bf16[5,1,48,16]{2,3,1,0:T(8,128)(2,1)S(1)} %get-tuple-element.18), channel_id=1, source_target_pairs={{0,1},{1,2},{2,3},{3,4},{4,5},{5,6},{6,7},{7,8},{8,9},{9,10},{10,1... | collective-permute-start | bytes 23048 | tf_op jit(solution)/shard_map/ppermute | solution.py:454
  143.0 17.6 %all-to-all-start = ((bf16[16,72,256]{2,1,0:T(8,128)(2,1)}), bf16[16,72,256]{2,1,0:T(8,128)(2,1)}, u32[]{:S(2)}, u32[]{:S(2)}) async-start(bf16[16,72,256]{2,1,0:T(8,128)(2,1)} %bitcast.43), calls=%async_computation | async-start | bytes 1179648 | tf_op jit(solution)/shard_map/all_to_all | solution.py:436
  160.6 0.9 copy-start.4
  (4 other events, 3.3 us)
Sparse Core Ops, SparseCore 0:
  34.7 54.4 all-gather.2
